TPU v7x, 256 devices: a whole 4x4x8 slice. The times are simulated.
256 devices in a mesh: row: 16 (over y_hi, z), col: 16 (over x, y_lo, core).
Axes of the slice: x: 4, y: 4 (y_hi: 2, y_lo: 2; y = y_hi * 2 + y_lo), z: 8, core: 2. Of those that a mesh axis runs over, the one named last changes fastest.
Arguments:
- factor: bfloat16 [16384, 16384], P('row', 'col'), may hold values from -0.078125 to 0.078125
- diag_inv: bfloat16 [16384, 1024], P('row'), may hold values from -1 to 1.5, as said below
- rhs: bfloat16 [16384, 256], P('row'), may hold values from -6 to 6
- forward_values: bfloat16 [16384, 256], P('row'), may hold values from -6 to 6
Outputs:
- forward_solved: bfloat16 [3072, 256], replicated
- forward_rest: float32 [16384, 256], P('row', 'col')
- back_sums: float32 [16384, 256], P('col', 'row')
- solution: float32 [16384, 256], P('row')
Inputs may be any that keep to these rules, and one draw needn't show every extreme that they name: Each 1024 x 1024 block of diag_inv is lower triangular with diagonal entries between 0.5 and 1.5.
All inputs are finite; a program needn't handle non-finite values.
Results may differ from a plain program's by a relative error of at most 0.0095.
Values may be sent and summed in bfloat16 or wider, within the bound.
A program may use at most 64 MiB of HBM per device.

v0:
```python
import jax
import jax.numpy as jnp
from jax import lax
from jax.sharding import PartitionSpec as P

NB = 1024
STEPS = 3


def broadcast(array, axis, root):
    mine = lax.axis_index(axis) == root
    return lax.psum(jnp.where(mine, array, jnp.zeros_like(array)), axis)


def local(factor, diag_inv, rhs, forward_values):
    row_blocks = factor.shape[0] // NB
    col_blocks = factor.shape[1] // NB
    columns = rhs.shape[1]
    row_count = lax.axis_size("row")
    col_count = lax.axis_size("col")
    my_row = lax.axis_index("row")
    my_col = lax.axis_index("col")
    block_total = row_blocks * row_count
    col_share = columns // col_count
    row_share = columns // row_count
    blocks = factor.reshape(row_blocks, NB, col_blocks, NB)
    inverses = diag_inv.reshape(row_blocks, NB, NB)
    right_sides = rhs.reshape(row_blocks, NB, columns)
    starting = forward_values.reshape(row_blocks, NB, columns)
    row_ids = my_row * row_blocks + jnp.arange(row_blocks, dtype=jnp.int32)
    col_ids = my_col * col_blocks + jnp.arange(col_blocks, dtype=jnp.int32)
    partial_value = jnp.zeros((row_blocks, NB, columns), jnp.float32)
    solved_list = []
    for position in range(STEPS):
        owner_row = position // row_blocks
        local_row = position % row_blocks
        owner_col = position // col_blocks
        local_col = position % col_blocks
        own_part = partial_value[local_row]
        inverse = inverses[local_row]
        right_side = right_sides[local_row]
        summed = lax.psum_scatter(
            own_part.astype(jnp.bfloat16), "col", scatter_dimension=1, tiled=True
        ).astype(jnp.float32)
        side_share = lax.dynamic_slice_in_dim(right_side, my_col * col_share, col_share, 1)
        residue = (side_share.astype(jnp.float32) - summed).astype(jnp.bfloat16)
        gathered = lax.all_gather(residue, "col", axis=1, tiled=True)

        def solve_whole(operand):
            return jnp.dot(inverse, operand, preferred_element_type=jnp.float32).astype(
                jnp.bfloat16
            )

        def skip_whole(operand):
            return jnp.zeros_like(operand)

        local_value = lax.cond(my_row == owner_row, solve_whole, skip_whole, gathered)
        solved_block = broadcast(local_value, "row", owner_row)
        solved_list.append(solved_block)

        def update(totals):
            column = blocks[:, :, local_col, :]
            update_term = jnp.einsum(
                "anm,mr->anr", column, solved_block, preferred_element_type=jnp.float32
            )
            later_rows = (row_ids > position)[:, None, None]
            return totals + jnp.where(later_rows, update_term, 0.0)

        def keep_same(totals):
            return totals

        partial_value = lax.cond(my_col == owner_col, update, keep_same, partial_value)
    rest_sum = lax.psum_scatter(
        partial_value.astype(jnp.bfloat16), "col", scatter_dimension=2, tiled=True
    ).astype(jnp.float32)
    side_part = lax.dynamic_slice_in_dim(right_sides, my_col * col_share, col_share, 2)
    forward_rest = (side_part.astype(jnp.float32) - rest_sum).reshape(row_blocks * NB, col_share)
    forward_solved = jnp.concatenate(solved_list, axis=0)
    back_partial = jnp.zeros((col_blocks, NB, columns), jnp.float32)
    result = jnp.zeros((row_blocks, NB, columns), jnp.float32)
    for reverse_turn in range(STEPS):
        position = block_total - 1 - reverse_turn
        owner_row = position // row_blocks
        local_row = position % row_blocks
        owner_col = position // col_blocks
        local_col = position % col_blocks
        own_part = back_partial[local_col]
        summed = lax.psum_scatter(
            own_part.astype(jnp.bfloat16), "row", scatter_dimension=1, tiled=True
        ).astype(jnp.float32)
        rounded = summed.astype(jnp.bfloat16)
        collected = lax.all_gather(rounded, "row", axis=1, tiled=True)
        gathered_sum = broadcast(collected, "col", owner_col)
        inverse = inverses[local_row]
        earlier = starting[local_row]
        current = result[local_row]
        row_block = blocks[local_row]

        def solve_back(totals):
            centred = (earlier.astype(jnp.float32) - gathered_sum.astype(jnp.float32)).astype(
                jnp.bfloat16
            )
            answer = lax.dot_general(
                inverse, centred, (((0,), (0,)), ((), ())), preferred_element_type=jnp.float32
            )
            update_term = jnp.einsum(
                "nbm,nr->bmr",
                row_block,
                answer.astype(jnp.bfloat16),
                preferred_element_type=jnp.float32,
            )
            earlier_cols = (col_ids < position)[:, None, None]
            return (answer, totals + jnp.where(earlier_cols, update_term, 0.0))

        def keep_back(totals):
            return (current, totals)

        answer, back_partial = lax.cond(my_row == owner_row, solve_back, keep_back, back_partial)
        result = result.at[local_row].set(answer)
    back_sums = (
        lax.psum_scatter(back_partial.astype(jnp.bfloat16), "row", scatter_dimension=2, tiled=True)
        .astype(jnp.float32)
        .reshape(col_blocks * NB, row_share)
    )
    return (forward_solved, forward_rest, back_sums, result.reshape(row_blocks * NB, columns))


def solution(mesh):
    placed = (P("row", "col"), P("row", None), P("row", None), P("row", None))
    return jax.shard_map(
        local,
        mesh=mesh,
        in_specs=placed,
        out_specs=(P(), P("row", "col"), P("col", "row"), P("row", None)),
        check_vma=False,
    )
```

profile of v0, /device:TPU:57, one launch (start us, length us, event | category | flops | bytes accessed | tf_op | source)
XLA Modules:
  0.0 1546.3 jit_solution(7506992182266080683)
XLA Ops:
  7.2 0.0 all-reduce.6.cloned.1.call-start
  7.2 1.0 copy-done
  8.2 0.1 constant_dynamic-slice_fusion
  8.4 0.1 copy.68
  8.5 18.7 %all_gather.16 = bf16[1024,256]{0,1:T(8,128)(2,1)S(1)} all-gather(bf16[1024,16]{0,1:T(8,128)(2,1)S(1)} %copy.68), channel_id=1, replica_groups=mesh['row'=16,'col'=16] {'col'}, dimensions={1}, use_global_device_ids=true | all-gather | bytes 557056 | tf_op jit(solution)/shard_map/all_gather | solution.py:47
  27.2 0.9 conditional.9
  27.2 0.9 broadcast.116.clone
  28.0 0.8 broadcast_select_fusion.4
  28.9 0.0 reduce-scatter.19.cloned.1.call-start
  28.9 0.9 broadcast.123
  29.8 0.0 copy-done.1
  29.8 2.2 conditional.15
  29.8 1.1 broadcast.120
  30.9 1.1 broadcast.121
  32.0 2.2 copy.42
  34.3 2.1 copy.56
  36.3 0.0 reduce-scatter.11.cloned.1.call-start
  36.4 138.1 %all-reduce.6.cloned.1.call-done = bf16[1024,256]{0,1:T(8,128)(2,1)} async-done(((bf16[1024,256]{0,1:T(8,128)(2,1)}), bf16[1024,256]{0,1:T(8,128)(2,1)}) %all-reduce.6.cloned.1.call-update) | async-done | bytes 524304 | tf_op jit(solution)/shard_map/psum | solution.py:12
  174.5 1.0 conditional.10
  174.5 1.0 broadcast.117
  175.5 2.2 copy.32
  177.8 0.0 all-reduce.12.cloned.1.call-start
  177.8 202.0 %reduce-scatter.19.cloned.1.call-done = bf16[16,1024]{1,0:T(8,128)(2,1)} async-done(((bf16[256,1024]{1,0:T(8,128)(2,1)}), bf16[16,1024]{1,0:T(8,128)(2,1)}) %reduce-scatter.19.cloned.1.call-update) | async-done | bytes 32784
  379.8 32.5 %all_gather.19 = bf16[1024,256]{0,1:T(8,128)(2,1)S(1)} all-gather(bf16[1024,16]{0,1:T(8,128)(2,1)} %bitcast.117), channel_id=1, replica_groups=mesh['row'=16,'col'=16] {'row'}, dimensions={1}, use_global_device_ids=true | all-gather | bytes 557056 | tf_op jit(solution)/shard_map/all_gather | solution.py:92
  412.3 0.8 broadcast_select_fusion.1
  413.2 0.0 all-reduce.8.cloned.1.call-start
  413.3 30.7 %reduce-scatter.11.cloned.1.call-done = bf16[1024,16]{0,1:T(8,128)(2,1)} async-done(((bf16[1024,256]{0,1:T(8,128)(2,1)}), bf16[1024,16]{0,1:T(8,128)(2,1)}) %reduce-scatter.11.cloned.1.call-update) | async-done | bytes 32784 | tf_op jit(solution)/shard_map/reduce_scatter | solution.py:42
  444.0 0.8 fusion.38
  444.8 25.6 %all_gather.17 = bf16[1024,256]{0,1:T(8,128)(2,1)S(1)} all-gather(bf16[1024,16]{0,1:T(8,128)(2,1)S(1)} %fusion.38), channel_id=1, replica_groups=mesh['row'=16,'col'=16] {'col'}, dimensions={1}, use_global_device_ids=true | all-gather | bytes 557056 | tf_op jit(solution)/shard_map/all_gather | solution.py:47
  470.4 0.9 conditional.11
  470.4 0.9 broadcast.118.clone
  471.2 0.8 broadcast_select_fusion.3
  472.1 0.0 reduce-scatter.21.cloned.1.call-start
  472.1 99.7 %all-reduce.12.cloned.1.call-done = bf16[1024,256]{0,1:T(8,128)(2,1)} async-done(((bf16[1024,256]{0,1:T(8,128)(2,1)}), bf16[1024,256]{0,1:T(8,128)(2,1)}) %all-reduce.12.cloned.1.call-update) | async-done | bytes 524304 | tf_op jit(solution)/shard_map/psum | solution.py:12
  571.8 2.2 copy.45
  574.0 2.1 copy.58
  576.1 0.0 reduce-scatter.13.cloned.1.call-start
  576.2 146.1 %all-reduce.8.cloned.1.call-done = bf16[1024,256]{0,1:T(8,128)(2,1)} async-done(((bf16[1024,256]{0,1:T(8,128)(2,1)}), bf16[1024,256]{0,1:T(8,128)(2,1)}) %all-reduce.8.cloned.1.call-update) | async-done | bytes 524304 | tf_op jit(solution)/shard_map/psum | solution.py:12
  722.3 2.2 copy.36
  724.5 0.0 all-reduce.14.cloned.1.call-start
  724.6 202.9 %reduce-scatter.21.cloned.1.call-done = bf16[16,1024]{1,0:T(8,128)(2,1)} async-done(((bf16[256,1024]{1,0:T(8,128)(2,1)}), bf16[16,1024]{1,0:T(8,128)(2,1)}) %reduce-scatter.21.cloned.1.call-update) | async-done | bytes 32784
  927.5 33.0 %all_gather.20 = bf16[1024,256]{0,1:T(8,128)(2,1)S(1)} all-gather(bf16[1024,16]{0,1:T(8,128)(2,1)} %bitcast.118), channel_id=1, replica_groups=mesh['row'=16,'col'=16] {'row'}, dimensions={1}, use_global_device_ids=true | all-gather | bytes 557056 | tf_op jit(solution)/shard_map/all_gather | solution.py:92
  960.4 0.8 broadcast_select_fusion
  961.3 0.0 all-reduce.10.cloned.1.call-start
  961.3 30.2 %reduce-scatter.13.cloned.1.call-done = bf16[1024,16]{0,1:T(8,128)(2,1)} async-done(((bf16[1024,256]{0,1:T(8,128)(2,1)}), bf16[1024,16]{0,1:T(8,128)(2,1)}) %reduce-scatter.13.cloned.1.call-update) | async-done | bytes 32784 | tf_op jit(solution)/shard_map/reduce_scatter | solution.py:42
  991.6 0.8 fusion.39
  992.3 25.7 %all_gather.18 = bf16[1024,256]{0,1:T(8,128)(2,1)S(1)} all-gather(bf16[1024,16]{0,1:T(8,128)(2,1)S(1)} %fusion.39), channel_id=1, replica_groups=mesh['row'=16,'col'=16] {'col'}, dimensions={1}, use_global_device_ids=true | all-gather | bytes 557056 | tf_op jit(solution)/shard_map/all_gather | solution.py:47
  1018.0 0.9 conditional.13
  1018.0 0.9 broadcast.119.clone
  1018.9 0.9 broadcast_select_fusion.2
  1019.7 0.0 reduce-scatter.17.cloned.1.call-start
  1019.8 99.8 %all-reduce.14.cloned.1.call-done = bf16[1024,256]{0,1:T(8,128)(2,1)} async-done(((bf16[1024,256]{0,1:T(8,128)(2,1)}), bf16[1024,256]{0,1:T(8,128)(2,1)}) %all-reduce.14.cloned.1.call-update) | async-done | bytes 524304 | tf_op jit(solution)/shard_map/psum | solution.py:12
  1119.6 2.5 conditional.17
  1119.6 2.5 copy.66
  1122.1 2.1 convert_element_type.164
  1124.2 0.0 reduce-scatter.15.cloned.1.call-start
  1124.3 145.3 %all-reduce.10.cloned.1.call-done = bf16[1024,256]{0,1:T(8,128)(2,1)} async-done(((bf16[1024,256]{0,1:T(8,128)(2,1)}), bf16[1024,256]{0,1:T(8,128)(2,1)}) %all-reduce.10.cloned.1.call-update) | async-done | bytes 524304 | tf_op jit(solution)/shard_map/psum | solution.py:12
  1269.6 2.3 copy.40
  1272.0 1.1 pad_maximum_fusion
  1273.2 1.6 copy.48
  1274.7 200.1 %reduce-scatter.17.cloned.1.call-done = bf16[1,1024,16]{1,2,0:T(8,128)(2,1)} async-done(((bf16[1,1024,256]{1,2,0:T(8,128)(2,1)}), bf16[1,1024,16]{1,2,0:T(8,128)(2,1)}) %reduce-scatter.17.cloned.1.call-update) | async-done | bytes 32784 | tf_op jit(solution)/shard_map/reduce_scatter | solution.py:121
  1474.8 1.4 bitcast_convert_fusion
  1476.2 62.1 %reduce-scatter.15.cloned.1.call-done = bf16[1,1024,16]{1,2,0:T(8,128)(2,1)} async-done(((bf16[1,1024,256]{1,2,0:T(8,128)(2,1)}), bf16[1,1024,16]{1,2,0:T(8,128)(2,1)}) %reduce-scatter.15.cloned.1.call-update) | async-done | bytes 32784 | tf_op jit(solution)/shard_map/reduce_scatter | solution.py:73
  1538.3 1.4 fusion.41
  (22 shorter events, 0.2 us)
Async XLA Ops:
  7.2 1.0 copy-start
  7.2 167.3 %all-reduce.6.cloned.1.call-start = ((), (), s32[]{:S(2)}) async-start(), calls=%async_computation.6 | async-start | bytes 1048576 | tf_op jit(solution)/shard_map/psum | solution.py:12
  27.1 2.6 copy-start.3
  28.0 1.8 copy-start.1
  28.9 350.9 %reduce-scatter.19.cloned.1.call-start = ((), (), s32[]{:S(2)}) async-start(), calls=%async_computation.15 | async-start | bytes 557056
  36.3 407.6 %reduce-scatter.11.cloned.1.call-start = ((), (), s32[]{:S(2)}) async-start(), calls=%async_computation.7 | async-start | bytes 557056 | tf_op jit(solution)/shard_map/reduce_scatter | solution.py:42
  177.8 394.0 %all-reduce.12.cloned.1.call-start = ((), (), s32[]{:S(2)}) async-start(), calls=%async_computation.12 | async-start | bytes 1048576 | tf_op jit(solution)/shard_map/psum | solution.py:12
  413.2 309.1 %all-reduce.8.cloned.1.call-start = ((), (), s32[]{:S(2)}) async-start(), calls=%async_computation.8 | async-start | bytes 1048576 | tf_op jit(solution)/shard_map/psum | solution.py:12
  472.1 455.4 %reduce-scatter.21.cloned.1.call-start = ((), (), s32[]{:S(2)}) async-start(), calls=%async_computation.16 | async-start | bytes 557056
  576.1 415.4 %reduce-scatter.13.cloned.1.call-start = ((), (), s32[]{:S(2)}) async-start(), calls=%async_computation.9 | async-start | bytes 557056 | tf_op jit(solution)/shard_map/reduce_scatter | solution.py:42
  724.5 395.1 %all-reduce.14.cloned.1.call-start = ((), (), s32[]{:S(2)}) async-start(), calls=%async_computation.13 | async-start | bytes 1048576 | tf_op jit(solution)/shard_map/psum | solution.py:12
  961.3 308.3 %all-reduce.10.cloned.1.call-start = ((), (), s32[]{:S(2)}) async-start(), calls=%async_computation.10 | async-start | bytes 1048576 | tf_op jit(solution)/shard_map/psum | solution.py:12
  1019.7 455.1 %reduce-scatter.17.cloned.1.call-start = ((), (), s32[]{:S(2)}) async-start(), calls=%async_computation.14 | async-start | bytes 557056 | tf_op jit(solution)/shard_map/reduce_scatter | solution.py:121
  1124.2 414.1 %reduce-scatter.15.cloned.1.call-start = ((), (), s32[]{:S(2)}) async-start(), calls=%async_computation.11 | async-start | bytes 557056 | tf_op jit(solution)/shard_map/reduce_scatter | solution.py:73
  1269.6 2.4 copy-start.4
  1269.6 2.4 copy-start.5
Sparse Core Ops, SparseCore 0:
  29.0 145.4 all-reduce.5
  178.8 200.9 reduce-scatter.18
  382.9 61.0 reduce-scatter.10
  446.6 125.1 all-reduce.11
  574.8 147.3 all-reduce.7
  726.4 201.0 reduce-scatter.20
  930.5 60.9 reduce-scatter.12
  994.4 125.1 all-reduce.13
  1122.2 147.3 all-reduce.9
  1273.8 201.0 reduce-scatter.16
  1477.3 60.9 reduce-scatter.14
where the time goes:
time: 1550 us
  waiting for transfers between devices  1360 us (88%)
  blocking collectives  135 us (9%)
  local copies, waits for them, and re-layouts  27.4 us (2%)
    psum x5, waiting for transfers between devices, broadcast(): return lax.psum(jnp.where(mine, array, jnp.zeros_like(array)), axis)  629 us
    unnamed x13, waiting for transfers between devices  405 us
    reduce_scatter x1, waiting for transfers between devices, local(): lax.psum_scatter(back_partial.astype(jnp.bfloat16), 'row', scatter_dimens...  200 us
    all_gather x3, blocking collectives, local(): gathered = lax.all_gather(residue, 'col', axis=1, tiled=True)  69.9 us
    all_gather x2, blocking collectives, local(): collected = lax.all_gather(rounded, 'row', axis=1, tiled=True)  65.5 us
    reduce_scatter x1, waiting for transfers between devices, local(): lax.psum_scatter(partial_value.astype(jnp.bfloat16), 'col', scatter_dimen...  62.1 us
    reduce_scatter x2, waiting for transfers between devices, local(): lax.psum_scatter(own_part.astype(jnp.bfloat16), 'col', scatter_dimension=...  60.9 us
  transfers between devices with their start and end apart: 11, of which 11 were waited for; matrix products, arithmetic and copies ran while one was open for 2% of the time, Pallas kernels for 0%

commit v1 on v0

v1 whole, which is shorter than its diff:
```python
import jax
import jax.numpy as jnp
from jax import lax
from jax.experimental import pallas as pl
from jax.experimental.pallas import tpu as pltpu
from jax.sharding import PartitionSpec as P

NB = 1024
COLS = 256
STEPS = 3
NROW = 16
NCOL = 16
PIECE = 16
CHUNK = 64
HALF = 512
MESH = pl.DeviceIdType.MESH
F32 = jnp.float32
BF16 = jnp.bfloat16


def product(left, right):
    return lax.dot_general(left, right, (((1,), (0,)), ((), ())), preferred_element_type=F32)


def loop(count, body):
    def step(index, carry):
        body(index)
        return carry

    lax.fori_loop(0, count, step, 0)


def kernel(
    factor, inverse, rhs, start,
    solved_out, rest_out, back_out, solution_out,
    lv, dv, bv, uv, lt, dt, bt, ut,
    yt, yc, pc, yr, pf, rp, qf, qr, qc, tb, wg, vf, vb, so, sl,
    ld_s, out_s,
    yc_r, pc_r, own_r, s3_r, s4_r, rp_r, qr_r, qc_r, tb_r, ag_r, sib_r,
    y0_s, s1_s, s2_s, s3_s, s4_s, pf_s, fw_s, ch_s, pc_s, qf_s, qc_s, tb_s, ag_s, sib_s,
):
    r = lax.axis_index("row")
    c = lax.axis_index("col")
    x = c // 4
    yl = (c // 2) % 2
    e = c % 2
    yh = r // 8
    z = r % 8
    y = 2 * yh + yl
    mine = 4 * x + y
    row0 = r == 0
    chain1 = (r == 1) & (c == 0)
    chain20 = (r == 2) & (c == 0)
    chain2 = (r == 2) & (c == 1)
    row13 = r == 13
    row14 = r == 14
    row15 = r == 15
    late = r >= 13
    back1 = (r == 14) & (c == 13)
    half = pl.multiple_of(e * HALF, HALF)

    def remote(src, dst, send, recv, row, col):
        return pltpu.make_async_remote_copy(
            src_ref=src, dst_ref=dst, send_sem=send, recv_sem=recv, device_id=(row, col), device_id_type=MESH
        )

    def got(ref, sem):
        remote(ref, ref, sem, sem, r, c).wait_recv()

    def sent(ref, sem):
        remote(ref, ref, sem, sem, r, c).wait_send()

    def rows(index, count):
        return pl.ds(pl.multiple_of(index * count, count), count)

    loads = [
        pltpu.make_async_copy(source, target, ld_s.at[index])
        for index, (source, target) in enumerate(((inverse, dv), (rhs, bv), (factor, lv), (start, uv)))
    ]
    for load in loads:
        load.start()
    barrier = pltpu.get_barrier_semaphore()

    def greet(row, col):
        pl.semaphore_signal(barrier, inc=1, device_id=(row, col), device_id_type=MESH)

    loop(15, lambda k: greet(r, lax.rem(c + 1 + k, 16)))
    loop(15, lambda k: greet(lax.rem(r + 1 + k, 16), c))
    loop(16, lambda k: greet(lax.rem(r + 8, 16), k))

    @pl.when(chain1)
    def _():
        greet(0, 2)
        greet(0, 4)
        greet(0, 12)

    @pl.when(chain2)
    def _():
        greet(1, 0)

    @pl.when(row14 & (c != 14))
    def _():
        greet(15, 14)

    @pl.when(row13 & (c != 13))
    def _():
        greet(15, 13)
        greet(14, 13)

    sl[...] = jnp.zeros_like(sl)
    loads[0].wait()
    loads[1].wait()

    @pl.when(row0)
    def _():
        value = jnp.dot(dv[...], bv[...], preferred_element_type=F32)
        yr[...] = value.astype(BF16).T

    bt[...] = bv[...].T
    loads[2].wait()
    loads[3].wait()

    @pl.when(late)
    def _():
        ut[...] = uv[...].T

    @pl.when(row15)
    def _():
        value = product(ut[...], dv[...])
        vf[...] = value
        vb[...] = value.astype(BF16)

        @pl.when(c < 15)
        def _():
            qf[...] = product(vb[...], lv[...]).astype(BF16)

    @pl.when(chain1 | chain2)
    def _():
        dt[...] = dv[...].T

    @pl.when((c < 3) & (r > c))
    def _():
        lt[...] = lv[...].T

    extra = jnp.where(
        ((r == 15) & ((c == 14) | (c == 13))) | back1,
        15,
        jnp.where(chain1 | (row0 & ((c == 2) | (c == 4) | (c == 12))), 1, 0),
    )
    pl.semaphore_wait(barrier, 46 + extra)

    def scatter_pf(chunk):
        for k in range(4):
            g = 4 * chunk + k

            @pl.when(g != c)
            def _():
                remote(pf.at[rows(g, PIECE)], rp.at[c], pf_s, rp_r.at[c], r, g).start()

    def scatter_qf(chunk):
        for k in range(4):
            h = 4 * chunk + k

            @pl.when(h != r)
            def _():
                remote(qf.at[rows(h, PIECE)], qr.at[r - 13], qf_s, qr_r.at[r - 13], h, c).start()

    def send_t(slot, row):
        def one(g):
            remote(qf.at[rows(g, PIECE)], tb.at[slot], tb_s, tb_r.at[slot], row, g).start()

        return one

    @pl.when(row0)
    def _():
        for col, chunk in ((0, 2), (4, 1), (12, 0), (2, 3)):

            @pl.when(c == col)
            def _():
                part = pl.ds(chunk * CHUNK, CHUNK)
                remote(yr.at[part], yc.at[part], y0_s, yc_r.at[chunk], 1, 0).start()

        other = 3 - y
        part = rows(4 * x + other, PIECE)
        remote(
            yr.at[part, pl.ds(half, HALF)], yt.at[0, part, pl.ds(half, HALF)], s1_s.at[0], own_r.at[0],
            8, 4 * x + 2 * (other - 2) + e,
        ).start()
        part = rows(mine, PIECE)
        yt[0, part, pl.ds(half, HALF)] = yr[part, pl.ds(half, HALF)]

    @pl.when(row15 & (c == 14))
    def _():
        def one(step):
            chunk = lax.rem(5 - step, 4)
            part = rows(chunk, CHUNK)
            remote(qf.at[part], qc.at[part], qc_s.at[chunk], qc_r.at[chunk], 14, 13).start()

        loop(4, one)
        loop(16, send_t(0, 14))

    @pl.when(row15 & (c == 13))
    def _():
        loop(16, send_t(0, 13))

    @pl.when(row15 & (c < 15))
    def _():
        loop(4, scatter_qf)

    def scatter_s1(j, chunk):
        for k in range(4):
            for side in range(2):
                part = pl.ds(pl.multiple_of(chunk * CHUNK + k * PIECE, PIECE), PIECE)
                lanes = pl.ds(side * HALF, HALF)
                row = (k // 2) * 8 + j
                col = 4 * chunk + (k % 2) * 2 + side
                own = (r == row) & (c == col)

                @pl.when(jnp.logical_not(own))
                def _():
                    remote(yr.at[part, lanes], yt.at[j, part, lanes], s1_s.at[chunk], own_r.at[j], row, col).start()

                @pl.when(own)
                def _():
                    yt[j, part, lanes] = yr[part, lanes]

    @pl.when(chain1)
    def _():
        def one(step):
            chunk = lax.rem(6 - step, 4)
            part = rows(chunk, CHUNK)
            got(yc.at[part], yc_r.at[chunk])
            partial = product(yc[part], lt[...]).astype(BF16)
            pf[part] = partial
            residue = (bt[part].astype(F32) - partial.astype(F32)).astype(BF16)
            yr[part] = product(residue, dt[...]).astype(BF16)
            remote(yr.at[part], yc.at[part], ch_s.at[chunk], yc_r.at[chunk], 2, 1).start()
            remote(yc.at[part], yc.at[part], fw_s.at[chunk], yc_r.at[chunk], 2, 0).start()

        loop(4, one)

        def rest(step):
            chunk = lax.rem(6 - step, 4)
            scatter_s1(1, chunk)
            scatter_pf(chunk)

        loop(4, rest)

    @pl.when(chain20)
    def _():
        def one(step):
            chunk = lax.rem(6 - step, 4)
            part = rows(chunk, CHUNK)
            got(yc.at[part], yc_r.at[chunk])
            pf[part] = product(yc[part], lt[...]).astype(BF16)
            remote(pf.at[part], pc.at[part], pc_s.at[chunk], pc_r.at[chunk], 2, 1).start()

        loop(4, one)
        loop(4, scatter_pf)

    @pl.when(chain2)
    def _():
        def one(step):
            chunk = lax.rem(6 - step, 4)
            part = rows(chunk, CHUNK)
            got(yc.at[part], yc_r.at[chunk])
            partial = product(yc[part], lt[...]).astype(BF16)
            pf[part] = partial
            got(pc.at[part], pc_r.at[chunk])
            total = pc[part].astype(F32) + partial.astype(F32)
            residue = (bt[part].astype(F32) - total).astype(BF16)
            yr[part] = product(residue, dt[...]).astype(BF16)
            scatter_s1(2, chunk)

        loop(4, one)
        loop(4, scatter_pf)

    @pl.when(back1)
    def _():
        def one(step):
            chunk = lax.rem(5 - step, 4)
            part = rows(chunk, CHUNK)
            got(qc.at[part], qc_r.at[chunk])
            centred = (ut[part].astype(F32) - qc[part].astype(F32)).astype(BF16)
            answer = product(centred, dv[...]).astype(BF16)
            qf[part] = product(answer, lv[...]).astype(BF16)
            for k in range(4):
                send_t(1, 13)(4 * chunk + k)

        loop(4, one)

    def spread(j):
        part = rows(mine, PIECE)
        lanes = pl.ds(half, HALF)
        block = yt.at[j, part, lanes]

        root = (chain1 if j == 1 else chain2 if j == 2 else row0)

        @pl.when(jnp.logical_not(root if j == 0 else root & (mine == 0) & (e == (j - 1))))
        def _():
            got(block, own_r.at[j])

        @pl.when(z == j)
        def _():
            def along(k):
                far = lax.rem(z + jnp.where(k == 0, 4, jnp.where(k < 4, k, k + 1)), 8)
                remote(block, block, s2_s, own_r.at[j], yh * 8 + far, c).start()

            loop(7, along)

        def across(k):
            to = lax.rem(mine + 1 + k, 16)
            row = ((to % 4) // 2) * 8 + z
            col = 4 * (to // 4) + 2 * (to % 2) + e
            remote(block, block, s3_s.at[j], s3_r.at[j, x], row, col).start()

        loop(15, across)

    def collect(j):
        lanes = pl.ds(half, HALF)

        def one(step):
            chunk = lax.rem(6 - step, 4)
            part = rows(chunk, CHUNK)

            @pl.when(chunk == x)
            def _():
                got(yt.at[j, pl.ds(0, 48), lanes], s3_r.at[j, chunk])

            @pl.when(chunk != x)
            def _():
                got(yt.at[j, part, lanes], s3_r.at[j, chunk])

            block = yt.at[j, part, lanes]
            remote(block, block, s4_s.at[j, chunk], s4_r.at[j, chunk], r, c + 1 - 2 * e).start()

        loop(4, one)

    def apply(j):
        other = pl.ds(pl.multiple_of(HALF - half, HALF), HALF)

        def one(step):
            chunk = lax.rem(6 - step, 4)
            part = rows(chunk, CHUNK)
            got(yt.at[j, part, other], s4_r.at[j, chunk])

            @pl.when((c == j) & (r >= 3))
            def _():
                pf[part] = product(yt[j, part], lt[...]).astype(BF16)
                scatter_pf(chunk)

        loop(4, one)
        whole = pl.ds(j * NB, NB)
        so[whole] = yt[j].T
        pltpu.make_async_copy(so.at[whole], solved_out.at[whole], out_s.at[j]).start()

    def centre():
        @pl.when(row14 | row13)
        def _():
            got(tb.at[0], tb_r.at[0])

            @pl.when(row13)
            def _():
                got(tb.at[1], tb_r.at[1])

            total = tb[0].astype(F32)
            total = total + jnp.where(row13, tb[1].astype(F32), 0.0)
            summed = total.astype(BF16).astype(F32)
            piece = (ut[rows(c, PIECE)].astype(F32) - summed).astype(BF16)
            wg[x, yl, e] = piece
            block = wg.at[x, yl, e]

            def one(k):
                to = lax.rem(2 * x + yl + 1 + k, 8)
                remote(block, block, ag_s, ag_r.at[x], r, 2 * to + e).start()

            loop(7, one)

    def gather():
        @pl.when(row14 | row13)
        def _():
            def one(step):
                chunk = lax.rem(5 - step, 4)

                @pl.when(chunk == x)
                def _():
                    got(wg.at[chunk, 0, e], ag_r.at[chunk])

                @pl.when(chunk != x)
                def _():
                    got(wg.at[chunk, :, e], ag_r.at[chunk])

                block = wg.at[chunk, :, e]
                remote(block, block, sib_s.at[chunk], sib_r.at[chunk], r, c + 1 - 2 * e).start()

            loop(4, one)

    def solve():
        @pl.when(row14 | row13)
        def _():
            def one(step):
                chunk = lax.rem(5 - step, 4)
                part = rows(chunk, CHUNK)
                got(wg.at[chunk, :, 1 - e], sib_r.at[chunk])
                answer = product(wg[chunk].reshape(CHUNK, NB), dv[...])
                vf[part] = answer

                @pl.when((c < r) & jnp.logical_not(back1))
                def _():
                    qf[part] = product(answer.astype(BF16), lv[...]).astype(BF16)
                    scatter_qf(chunk)

            loop(4, one)

            @pl.when(back1)
            def _():
                loop(4, scatter_qf)

    spread(0)
    centre()
    collect(0)
    spread(1)
    gather()
    apply(0)
    solve()
    collect(1)
    apply(1)
    spread(2)
    collect(2)

    @pl.when(late)
    def _():
        sl[...] = vf[...].T

    done = pltpu.make_async_copy(sl, solution_out, out_s.at[3])
    done.start()
    apply(2)

    rest_out[...] = bt[rows(c, PIECE)].astype(F32)
    for j in range(STEPS):

        @pl.when(r > j)
        def _():
            @pl.when(c == j)
            def _():
                rest_out[...] -= pf[rows(c, PIECE)].astype(F32)

            @pl.when(c != j)
            def _():
                got(rp.at[j], rp_r.at[j])
                rest_out[...] -= rp[j].astype(F32)

    back_out[...] = jnp.zeros_like(back_out)
    for j in range(STEPS):

        @pl.when(c < 13 + j)
        def _():
            @pl.when(r == 13 + j)
            def _():
                back_out[...] += qf[rows(r, PIECE)].astype(F32)

            @pl.when(r != 13 + j)
            def _():
                got(qr.at[j], qr_r.at[j])
                back_out[...] += qr[j].astype(F32)

    lanes = pl.ds(0, HALF)
    for j in range(STEPS):
        sent(yt.at[j, pl.ds(0, 240), lanes], s3_s.at[j])
        loop(4, lambda k: sent(yt.at[j, pl.ds(0, CHUNK), lanes], s4_s.at[j, k]))

    @pl.when(z < STEPS)
    def _():
        sent(yt.at[0, pl.ds(0, 112), lanes], s2_s)

    @pl.when(row0)
    def _():
        @pl.when((c == 0) | (c == 2) | (c == 4) | (c == 12))
        def _():
            sent(yr.at[pl.ds(0, CHUNK)], y0_s)

        sent(yr.at[pl.ds(0, PIECE), lanes], s1_s.at[0])

    @pl.when(chain1 | chain2)
    def _():
        sent(yr.at[pl.ds(0, 112), lanes], s1_s.at[0])
        for k in range(1, 4):
            sent(yr.at[pl.ds(0, 128), lanes], s1_s.at[k])

    @pl.when(chain1)
    def _():
        for k in range(4):
            sent(yr.at[pl.ds(0, CHUNK)], ch_s.at[k])
            sent(yc.at[pl.ds(0, CHUNK)], fw_s.at[k])

    @pl.when(chain20)
    def _():
        for k in range(4):
            sent(pf.at[pl.ds(0, CHUNK)], pc_s.at[k])

    @pl.when((c < STEPS) & (r > c))
    def _():
        sent(pf.at[pl.ds(0, 240)], pf_s)

    @pl.when(late & (c < r))
    def _():
        sent(qf.at[pl.ds(0, 240)], qf_s)

    @pl.when(row15 & (c == 14))
    def _():
        for k in range(4):
            sent(qf.at[pl.ds(0, CHUNK)], qc_s.at[k])

    @pl.when((row15 & ((c == 14) | (c == 13))) | back1)
    def _():
        sent(qf, tb_s)

    @pl.when(row14 | row13)
    def _():
        sent(qf.at[pl.ds(0, 112)], ag_s)
        for k in range(4):
            sent(wg.at[0, :, 0], sib_s.at[k])

    for j in range(STEPS):
        whole = pl.ds(j * NB, NB)
        pltpu.make_async_copy(so.at[whole], solved_out.at[whole], out_s.at[j]).wait()
    done.wait()


def local(factor, diag_inv, rhs, forward_values):
    anywhere = pl.BlockSpec(memory_space=pl.ANY)
    vmem = pl.BlockSpec(memory_space=pltpu.VMEM)
    dma = pltpu.SemaphoreType.DMA
    square = pltpu.VMEM((NB, NB), BF16)
    tall = pltpu.VMEM((NB, COLS), BF16)
    wide = pltpu.VMEM((COLS, NB), BF16)
    solved, rest, back, answer = pl.pallas_call(
        kernel,
        name="solves",
        out_shape=(
            jax.ShapeDtypeStruct((STEPS * NB, COLS), BF16),
            jax.ShapeDtypeStruct((PIECE, NB), F32),
            jax.ShapeDtypeStruct((PIECE, NB), F32),
            jax.ShapeDtypeStruct((NB, COLS), F32),
        ),
        in_specs=[anywhere] * 4,
        out_specs=(anywhere, vmem, vmem, anywhere),
        scratch_shapes=[
            square, square, tall, tall, square, square, wide, wide,
            pltpu.VMEM((STEPS, COLS, NB), BF16),
            wide, wide, wide, wide,
            pltpu.VMEM((STEPS, PIECE, NB), BF16),
            wide,
            pltpu.VMEM((STEPS, PIECE, NB), BF16),
            wide,
            pltpu.VMEM((2, PIECE, NB), BF16),
            pltpu.VMEM((4, 2, 2, PIECE, NB), BF16),
            pltpu.VMEM((COLS, NB), F32),
            wide,
            pltpu.VMEM((STEPS * NB, COLS), BF16),
            pltpu.VMEM((NB, COLS), F32),
            dma((4,)), dma((4,)),
            dma((4,)), dma((4,)), dma((3,)), dma((3, 4)), dma((3, 4)), dma((3,)), dma((3,)), dma((4,)), dma((2,)),
            dma((4,)), dma((4,)),
            dma(()), dma((4,)), dma(()), dma((3,)), dma((3, 4)), dma(()), dma((4,)), dma((4,)), dma((4,)),
            dma(()), dma((4,)), dma(()), dma(()), dma((4,)),
        ],
        compiler_params=pltpu.CompilerParams(
            collective_id=0, has_side_effects=True, vmem_limit_bytes=48 * 1024 * 1024
        ),
    )(factor, diag_inv, rhs, forward_values)
    return solved, rest.T, back.T, answer


def solution(mesh):
    placed = (P("row", "col"), P("row", None), P("row", None), P("row", None))
    return jax.shard_map(
        local,
        mesh=mesh,
        in_specs=placed,
        out_specs=(P(), P("row", "col"), P("col", "row"), P("row", None)),
        check_vma=False,
    )
```

time: 1550 us -> 71.2 us (0.05)
  the two profiles are of different devices: /device:TPU:57 before, /device:TPU:23 now
where the time goes in v1:
time: 71.2 us; the launch traced here: 71 us
  Pallas kernels  63.3 us (89%)
  local copies, waits for them, and re-layouts  7.04 us (10%)
    pallas_call x1, Pallas kernels, local(): pl.pallas_call(kernel, name='solves', out_shape=(jax.ShapeDtypeStruct((ST...  63.3 us
    unnamed x10, local copies, waits for them, and re-layouts  7.04 us

profile of v1, /device:TPU:23, one launch (start us, length us, event | category | flops | bytes accessed | tf_op | source)
XLA Modules:
  0.0 71.0 jit_solution(764232663360255153)
XLA Ops:
  0.6 0.0 copy-start
  0.6 1.6 %copy-done = bf16[1024,1024]{1,0:T(8,128)(2,1)S(1)} copy-done((bf16[1024,1024]{1,0:T(8,128)(2,1)S(1)}, bf16[1024,1024]{1,0:T(8,128)(2,1)}, u32[]{:S(2)}) %copy-start) | copy-done | bytes 2097176
  2.2 0.0 copy-start.1
  2.2 1.0 %copy-done.1 = bf16[1024,256]{1,0:T(8,128)(2,1)S(1)} copy-done((bf16[1024,256]{1,0:T(8,128)(2,1)S(1)}, bf16[1024,256]{1,0:T(8,128)(2,1)}, u32[]{:S(2)}) %copy-start.1) | copy-done | bytes 524312
  3.3 0.0 copy-start.2
  3.3 1.0 %copy-done.2 = bf16[1024,256]{1,0:T(8,128)(2,1)S(1)} copy-done((bf16[1024,256]{1,0:T(8,128)(2,1)S(1)}, bf16[1024,256]{1,0:T(8,128)(2,1)}, u32[]{:S(2)}) %copy-start.2) | copy-done | bytes 524312
  4.3 63.3 %solves.1 = (bf16[3072,256]{1,0:T(8,128)(2,1)S(1)}, f32[16,1024]{1,0:T(8,128)S(1)}, f32[16,1024]{1,0:T(8,128)S(1)}, f32[1024,256]{1,0:T(8,128)S(1)}) custom-call(bf16[1024,1024]{1,0:T(8,128)(2,1)S(1)} %copy-done, bf16[1024,1024]{1,0:T(8,128)(2,1)} %inverse.1, bf16[1024,256]{1,0:T(8,128)(2,1)S(1)} %copy-done.1, bf16[1024,256]{1,0:T(8,128)(2,1)S(1)} %copy-done.2), custom_call_target="tpu_custom_call" | custom-call | tf_op jit(solution)/shard_map/solves/pallas_call | solution.py:537
  67.6 1.1 %copy.12 = bf16[3072,256]{1,0:T(8,128)(2,1)} copy(bf16[3072,256]{1,0:T(8,128)(2,1)S(1)} %get-tuple-element.16) | data formatting | bytes 3145728
  68.7 0.6 copy.13
  69.4 0.6 copy.14
  70.0 1.0 %copy.15 = f32[1024,256]{1,0:T(8,128)} copy(f32[1024,256]{1,0:T(8,128)S(1)} %get-tuple-element.19) | data formatting | bytes 2097152
Async XLA Ops:
  0.6 1.6 %copy-start = (bf16[1024,1024]{1,0:T(8,128)(2,1)S(1)}, bf16[1024,1024]{1,0:T(8,128)(2,1)}, u32[]{:S(2)}) copy-start(bf16[1024,1024]{1,0:T(8,128)(2,1)} %factor.1) | copy-start | bytes 6291460
  2.2 1.0 %copy-start.1 = (bf16[1024,256]{1,0:T(8,128)(2,1)S(1)}, bf16[1024,256]{1,0:T(8,128)(2,1)}, u32[]{:S(2)}) copy-start(bf16[1024,256]{1,0:T(8,128)(2,1)} %rhs.1) | copy-start | bytes 1572868
  3.3 1.0 %copy-start.2 = (bf16[1024,256]{1,0:T(8,128)(2,1)S(1)}, bf16[1024,256]{1,0:T(8,128)(2,1)}, u32[]{:S(2)}) copy-start(bf16[1024,256]{1,0:T(8,128)(2,1)} %start.1) | copy-start | bytes 1572868

commit v2 on v1

v2 whole, which is shorter than its diff:
```python
import jax
import jax.numpy as jnp
from jax import lax
from jax.experimental import pallas as pl
from jax.experimental.pallas import tpu as pltpu
from jax.sharding import PartitionSpec as P

NB = 1024
COLS = 256
STEPS = 3
NROW = 16
NCOL = 16
PIECE = 16
CHUNK = 64
HALF = 512
MESH = pl.DeviceIdType.MESH
F32 = jnp.float32
BF16 = jnp.bfloat16


def product(left, right):
    return lax.dot_general(left, right, (((1,), (0,)), ((), ())), preferred_element_type=F32)


def loop(count, body):
    def step(index, carry):
        body(index)
        return carry

    lax.fori_loop(0, count, step, 0)


def kernel(
    factor, inverse, rhs, start,
    solved_out, rest_out, back_out, solution_out,
    lv, dv, bv, uv, lt, dt, bt, ut,
    yt, yc, pc, yr, pf, rp, qf, qr, qc, tb, wg, vf, vb,
    ready, ld_s, out_s,
    yc_r, pc_r, own_r, s3_r, s4_r, rp_r, qr_r, qc_r, tb_r, ag_r, sib_r,
    y0_s, s1_s, s1b_s, s2_s, s3_s, s4_s, pf_s, ch_s, pc_s, qf_s, qc_s, tb_s, ag_s, sib_s,
):
    r = lax.axis_index("row")
    c = lax.axis_index("col")
    x = c // 4
    yl = (c // 2) % 2
    e = c % 2
    yh = r // 8
    z = r % 8
    y = 2 * yh + yl
    row0 = r == 0
    chain1 = (r == 1) & (c == 0)
    chain20 = (r == 2) & (c == 0)
    chain2 = (r == 2) & (c == 1)
    row13 = r == 13
    row14 = r == 14
    row15 = r == 15
    late = r >= 13
    first = jnp.where(e == 0, (x < 2) & (y < 2), ((x == 0) | (x == 3)) & ((y == 0) | (y == 3)))
    back1 = (r == 14) & (c == 13)
    half = pl.multiple_of(e * HALF, HALF)
    lanes = pl.ds(half, HALF)
    group = 2 * (x % 2) + y % 2
    mine = pl.ds(pl.multiple_of(group * CHUNK, CHUNK), CHUNK)

    def remote(src, dst, send, recv, row, col):
        return pltpu.make_async_remote_copy(
            src_ref=src, dst_ref=dst, send_sem=send, recv_sem=recv, device_id=(row, col), device_id_type=MESH
        )

    def got(ref, sem):
        remote(ref, ref, sem, sem, r, c).wait_recv()

    def sent(ref, sem):
        remote(ref, ref, sem, sem, r, c).wait_send()

    def rows(index, count):
        return pl.ds(pl.multiple_of(index * count, count), count)

    uses_l = ((c < STEPS) & (r > c)) | (late & (c < r))
    uses_d = row0 | chain1 | chain2 | late
    needs = (uses_d, r >= 0, uses_l, late)
    pairs = ((inverse, dv), (rhs, bv), (factor, lv), (start, uv))
    loads = [pltpu.make_async_copy(source, target, ld_s.at[k]) for k, (source, target) in enumerate(pairs)]
    for need, load in zip(needs, loads):
        pl.when(need)(load.start)
    barrier = pltpu.get_barrier_semaphore()

    def greet(row, col):
        pl.semaphore_signal(barrier, inc=1, device_id=(row, col), device_id_type=MESH)

    def greet_other(row, col):
        pl.when((row != r) | (col != c))(lambda: greet(row, col))

    @pl.when(chain1)
    def _():
        for col in (0, 2, 4, 12):
            greet(0, col)

    @pl.when(chain20)
    def _():
        for col in (6, 8, 13, 14):
            greet(0, col)

    @pl.when(chain2)
    def _():
        greet(1, 0)

    pl.when(z == 1)(lambda: greet_other(1, 0))
    pl.when(z == 2)(lambda: greet_other(2, 1))
    greet(r, c + 1 - 2 * e)
    loop(7, lambda k: greet(r, lax.rem(c + 2 + 2 * k, 16)))
    loop(8, lambda k: greet(lax.rem(r + 8, 16), 2 * k + e))
    for col in range(STEPS):
        pl.when(c != col)(lambda: greet(r, col))
    pl.when(r != 13)(lambda: greet(13, c))
    pl.when(r != 14)(lambda: greet(14, c))
    pl.when(r != 15)(lambda: greet(15, c))
    def depth(j):
        return lax.rem(z - j + 8, 8)

    def column(j, far):
        return yh * 8 + lax.rem(far + j, 8)

    def with_children(j, run):
        for parent, children in ((0, (3, 1, 7)), (3, (5, 4, 2)), (7, (6,))):

            @pl.when(depth(j) == parent)
            def _():
                run(children)

    for j in range(STEPS):
        with_children(j, lambda children: [greet(column(j, far), c) for far in children])

    @pl.when(row14 & (c != 14))
    def _():
        greet(15, 14)

    @pl.when(row13 & (c != 13))
    def _():
        greet(15, 13)
        greet(14, 13)

    pl.when(uses_d)(loads[0].wait)
    loads[1].wait()

    @pl.when(row0)
    def _():
        value = jnp.dot(dv[...], bv[...], preferred_element_type=F32)
        yr[...] = value.astype(BF16).T

    bt[...] = bv[...].T
    pl.when(uses_l)(loads[2].wait)

    @pl.when(late)
    def _():
        loads[3].wait()
        ut[...] = uv[...].T

    @pl.when(row15)
    def _():
        value = product(ut[...], dv[...])
        vf[...] = value
        vb[...] = value.astype(BF16)

        @pl.when(c < 15)
        def _():
            qf[...] = product(vb[...], lv[...]).astype(BF16)

    @pl.when(chain1 | chain2)
    def _():
        dt[...] = dv[...].T

    @pl.when((c < 3) & (r > c))
    def _():
        lt[...] = lv[...].T

    def source_of(cols):
        found = c == cols[0]
        for col in cols[1:]:
            found = found | (c == col)
        return row0 & found

    to_one = source_of((0, 2, 4, 12))
    to_two = source_of((6, 8, 13, 14))
    count = 16 + jnp.where(c < STEPS, 15, 0) + jnp.where(z < STEPS, 2, 3) + jnp.where(late, 15, 0)
    count = count + jnp.where(chain1 | chain2, 31, 0)
    count = count + jnp.where(to_one | to_two | chain1, 1, 0)
    count = count + jnp.where((row15 & ((c == 14) | (c == 13))) | back1, 15, 0)
    pl.semaphore_wait(barrier, count)

    for j in range(STEPS):
        near = jnp.where(depth(j) == 6, 7, jnp.where((depth(j) == 1) | (depth(j) == 3) | (depth(j) == 7), 0, 3))

        @pl.when(depth(j) != 0)
        def _():
            pl.semaphore_signal(ready.at[j], inc=1, device_id=(column(j, near), c), device_id_type=MESH)

    def scatter_pf(chunk):
        for k in range(4):
            g = 4 * chunk + k

            @pl.when(g != c)
            def _():
                remote(pf.at[rows(g, PIECE)], rp.at[c], pf_s, rp_r.at[c], r, g).start()

    def scatter_qf(chunk):
        for k in range(4):
            h = 4 * chunk + k

            @pl.when(h != r)
            def _():
                remote(qf.at[rows(h, PIECE)], qr.at[r - 13], qf_s, qr_r.at[r - 13], h, c).start()

    def send_t(slot, row):
        def one(g):
            remote(qf.at[rows(g, PIECE)], tb.at[slot], tb_s, tb_r.at[slot], row, g).start()

        return one

    @pl.when(row0)
    def _():
        for col, chunk in ((0, 3), (4, 2), (12, 1), (2, 0)):

            @pl.when(c == col)
            def _():
                part = pl.ds(chunk * CHUNK, CHUNK)
                remote(yr.at[part], yc.at[part], y0_s, yc_r.at[chunk], 1, 0).start()

        for col, chunk in ((6, 3), (8, 2), (14, 1), (13, 0)):

            @pl.when(c == col)
            def _():
                part = pl.ds(chunk * CHUNK, CHUNK)
                remote(yr.at[part], yc.at[part], y0_s, yc_r.at[chunk], 2, 0).start()

        other = 3 - y
        part = rows(2 * (x % 2) + other % 2, CHUNK)
        remote(yr.at[part, lanes], yt.at[0, part, lanes], s1_s.at[0], own_r.at[0], 8, 4 * x + 2 * (other - 2) + e).start()
        yt[0, mine, lanes] = yr[mine, lanes]

    @pl.when(row15 & (c == 14))
    def _():
        def one(step):
            chunk = lax.rem(5 - step, 4)
            part = rows(chunk, CHUNK)
            remote(qf.at[part], qc.at[part], qc_s.at[chunk], qc_r.at[chunk], 14, 13).start()

        loop(4, one)
        for k in range(4):
            sent(qf.at[pl.ds(0, CHUNK)], qc_s.at[k])
        loop(16, send_t(0, 14))

    @pl.when(row15 & (c == 13))
    def _():
        loop(16, send_t(0, 13))

    def scatter_s1(j, chunk):
        part = rows(chunk, CHUNK)
        a, b = chunk // 2, chunk % 2
        for side in range(2):
            far = pl.ds(side * HALF, HALF)
            row = j + (8 * b if side else 0)
            col = (12 * a + 2 * b + 1) if side else (4 * a + 2 * b)
            own = (r == row) & (c == col)

            @pl.when(jnp.logical_not(own))
            def _():
                remote(yr.at[part, far], yt.at[j, part, far], s1_s.at[chunk], own_r.at[j], row, col).start()

            @pl.when(own)
            def _():
                yt[j, part, far] = yr[part, far]

    def spread(step):
        j = jnp.where(z == 1, (1, 0, 2)[step], jnp.where(z == 2, (2, 0, 1)[step], step))
        block = yt.at[j, mine, lanes]
        local = (row0 & (j == 0)) | (chain1 & (j == 1)) | (chain2 & (j == 2))

        @pl.when(jnp.logical_not(local))
        def _():
            got(block, own_r.at[j])

        def to_chip(send, recv, tx, ty):
            remote(block, block, send, recv, 8 * (ty // 2) + z, 4 * tx + 2 * (ty % 2) + e).start()

        @pl.when((z == j) & (j > 0) & first)
        def _():
            x2, y2 = lax.rem(x + 2, 4), lax.rem(y + 2, 4)
            to_chip(s1b_s, own_r.at[j], x2, y2)
            to_chip(s1b_s, own_r.at[j], x2, y)
            to_chip(s1b_s, own_r.at[j], x, y2)

        x1, y1 = lax.rem(x + 1 + 2 * e, 4), lax.rem(y + 1 + 2 * e, 4)
        to_chip(s3_s.at[j], s3_r.at[j, group], x1, y1)
        to_chip(s3_s.at[j], s3_r.at[j, group], x1, y)
        to_chip(s3_s.at[j], s3_r.at[j, group], x, y1)
        remote(block, block, s4_s.at[j], s4_r.at[j, group], r, c + 1 - 2 * e).start()

        def run(children):
            pl.semaphore_wait(ready.at[j], len(children))
            for far in children:
                remote(block, block, s2_s.at[j], own_r.at[j], column(j, far), c).start()

        with_children(j, run)

    def collect(j):
        def one(step):
            chunk = 3 - step
            block = yt.at[j, rows(chunk, CHUNK), lanes]

            @pl.when(chunk != group)
            def _():
                got(block, s3_r.at[j, chunk])
                remote(block, block, s4_s.at[j], s4_r.at[j, chunk], r, c + 1 - 2 * e).start()

        loop(4, one)

    def apply(j):
        other = pl.ds(pl.multiple_of(HALF - half, HALF), HALF)

        def one(step):
            chunk = 3 - step
            part = rows(chunk, CHUNK)
            got(yt.at[j, part, other], s4_r.at[j, chunk])

            @pl.when((c == j) & (r >= 3))
            def _():
                partial = product(yt[j, part], lt[...]).astype(BF16)
                if j == 1:
                    got(pc.at[part], pc_r.at[chunk])
                    partial = (pc[part].astype(F32) + partial.astype(F32)).astype(BF16)
                pf[part] = partial
                if j == 0:
                    remote(pf.at[part], pc.at[part], pc_s.at[chunk], pc_r.at[chunk], r, 1).start()
                else:
                    scatter_pf(chunk)

        loop(4, one)
        pltpu.make_async_copy(yt.at[j], solved_out.at[j], out_s.at[j]).start()

    def centre():
        @pl.when(row14 | row13)
        def _():
            got(tb.at[0], tb_r.at[0])

            @pl.when(row13)
            def _():
                got(tb.at[1], tb_r.at[1])

            total = tb[0].astype(F32)
            total = total + jnp.where(row13, tb[1].astype(F32), 0.0)
            summed = total.astype(BF16).astype(F32)
            piece = (ut[rows(c, PIECE)].astype(F32) - summed).astype(BF16)
            wg[x, yl, e] = piece
            block = wg.at[x, yl, e]

            def one(k):
                to = lax.rem(2 * x + yl + 1 + k, 8)
                remote(block, block, ag_s, ag_r.at[x], r, 2 * to + e).start()

            loop(7, one)

    def gather():
        @pl.when(row14 | row13)
        def _():
            def one(step):
                chunk = lax.rem(5 - step, 4)

                @pl.when(chunk == x)
                def _():
                    got(wg.at[chunk, 0, e], ag_r.at[chunk])

                @pl.when(chunk != x)
                def _():
                    got(wg.at[chunk, :, e], ag_r.at[chunk])

                block = wg.at[chunk, :, e]
                remote(block, block, sib_s.at[chunk], sib_r.at[chunk], r, c + 1 - 2 * e).start()

            loop(4, one)

    def solve():
        @pl.when(row14 | row13)
        def _():
            def one(step):
                chunk = lax.rem(5 - step, 4)
                part = rows(chunk, CHUNK)
                got(wg.at[chunk, :, 1 - e], sib_r.at[chunk])
                answer = product(wg[chunk].reshape(CHUNK, NB), dv[...])
                vf[part] = answer

                @pl.when((c < r) & jnp.logical_not(back1))
                def _():
                    qf[part] = product(answer.astype(BF16), lv[...]).astype(BF16)
                    scatter_qf(chunk)

            loop(4, one)

            @pl.when(back1)
            def _():
                loop(4, scatter_qf)

    @pl.when(chain1)
    def _():
        def one(step):
            chunk = 3 - step
            part = rows(chunk, CHUNK)
            got(yc.at[part], yc_r.at[chunk])
            partial = product(yc[part], lt[...]).astype(BF16)
            pf[part] = partial
            residue = (bt[part].astype(F32) - partial.astype(F32)).astype(BF16)
            yr[part] = product(residue, dt[...]).astype(BF16)
            remote(yr.at[part], yc.at[part], ch_s.at[chunk], yc_r.at[chunk], 2, 1).start()
            for k in range(4):
                pl.when(chunk == k)(lambda: scatter_s1(1, k))

        loop(4, one)

    @pl.when(chain20)
    def _():
        def one(step):
            chunk = 3 - step
            part = rows(chunk, CHUNK)
            got(yc.at[part], yc_r.at[chunk])
            pf[part] = product(yc[part], lt[...]).astype(BF16)
            remote(pf.at[part], pc.at[part], pc_s.at[chunk], pc_r.at[chunk], 2, 1).start()

        loop(4, one)

    @pl.when(chain2)
    def _():
        def one(step):
            chunk = 3 - step
            part = rows(chunk, CHUNK)
            got(yc.at[part], yc_r.at[chunk])
            partial = product(yc[part], lt[...]).astype(BF16)
            got(pc.at[part], pc_r.at[chunk])
            total = pc[part].astype(F32) + partial.astype(F32)
            pf[part] = total.astype(BF16)
            residue = (bt[part].astype(F32) - total).astype(BF16)
            yr[part] = product(residue, dt[...]).astype(BF16)
            for k in range(4):
                pl.when(chunk == k)(lambda: scatter_s1(2, k))

        loop(4, one)

    @pl.when(back1)
    def _():
        def one(step):
            chunk = lax.rem(5 - step, 4)
            part = rows(chunk, CHUNK)
            got(qc.at[part], qc_r.at[chunk])
            centred = (ut[part].astype(F32) - qc[part].astype(F32)).astype(BF16)
            answer = product(centred, dv[...]).astype(BF16)
            qf[part] = product(answer, lv[...]).astype(BF16)
            for k in range(4):
                send_t(1, 13)(4 * chunk + k)

        loop(4, one)

    spread(0)

    @pl.when(row15 & (c < 15))
    def _():
        loop(4, scatter_qf)

    spread(1)
    centre()
    collect(0)
    apply(0)
    gather()
    spread(2)
    solve()

    @pl.when(chain1 | chain2)
    def _():
        loop(4, scatter_pf)

    collect(1)
    apply(1)
    collect(2)
    done = pltpu.make_async_copy(vf, solution_out, out_s.at[3])
    pl.when(late)(done.start)
    apply(2)

    rest_out[...] = bt[rows(c, PIECE)].astype(F32)
    for j in range(STEPS):

        @pl.when((r == 1) if j == 0 else (r > j))
        def _():
            @pl.when(c == j)
            def _():
                rest_out[...] -= pf[rows(c, PIECE)].astype(F32)

            @pl.when(c != j)
            def _():
                got(rp.at[j], rp_r.at[j])
                rest_out[...] -= rp[j].astype(F32)

    back_out[...] = jnp.zeros_like(back_out)
    for j in range(STEPS):

        @pl.when(c < 13 + j)
        def _():
            @pl.when(r == 13 + j)
            def _():
                back_out[...] += qf[rows(r, PIECE)].astype(F32)

            @pl.when(r != 13 + j)
            def _():
                got(qr.at[j], qr_r.at[j])
                back_out[...] += qr[j].astype(F32)

    side = pl.ds(0, HALF)
    for j in range(STEPS):
        sent(yt.at[j, pl.ds(0, 192), side], s3_s.at[j])
        sent(yt.at[j, :, side], s4_s.at[j])
        with_children(j, lambda children: sent(yt.at[j, pl.ds(0, len(children) * CHUNK), side], s2_s.at[j]))

    @pl.when(((z == 1) | (z == 2)) & first)
    def _():
        sent(yt.at[0, pl.ds(0, 192), side], s1b_s)

    @pl.when(row0)
    def _():
        @pl.when(to_one | to_two)
        def _():
            sent(yr.at[pl.ds(0, CHUNK)], y0_s)

        sent(yr.at[pl.ds(0, CHUNK), side], s1_s.at[0])

    @pl.when(chain1 | chain2)
    def _():
        sent(yr.at[pl.ds(0, CHUNK), side], s1_s.at[0])
        for k in range(1, 4):
            sent(yr.at[pl.ds(0, 2 * CHUNK), side], s1_s.at[k])

    @pl.when(chain1)
    def _():
        for k in range(4):
            sent(yr.at[pl.ds(0, CHUNK)], ch_s.at[k])

    @pl.when((c == 0) & (r >= 2))
    def _():
        for k in range(4):
            sent(pf.at[pl.ds(0, CHUNK)], pc_s.at[k])

    @pl.when(chain1 | ((c == 1) & (r >= 2)) | ((c == 2) & (r >= 3)))
    def _():
        sent(pf.at[pl.ds(0, 240)], pf_s)

    @pl.when(late & (c < r))
    def _():
        sent(qf.at[pl.ds(0, 240)], qf_s)

    @pl.when((row15 & ((c == 14) | (c == 13))) | back1)
    def _():
        sent(qf, tb_s)

    @pl.when(row14 | row13)
    def _():
        sent(qf.at[pl.ds(0, 112)], ag_s)
        for k in range(4):
            sent(wg.at[0, :, 0], sib_s.at[k])

    for j in range(STEPS):
        pltpu.make_async_copy(yt.at[j], solved_out.at[j], out_s.at[j]).wait()
    pl.when(late)(done.wait)


def hand_over(yt, rest, back, vf, solved_out, rest_out, back_out, solution_out, yv, so, rv, bv, sv, sl, in_s, out_s):
    late = lax.axis_index("row") >= 13
    loads = [pltpu.make_async_copy(yt.at[j], yv.at[j], in_s.at[j]) for j in range(STEPS)]
    loads += [pltpu.make_async_copy(rest, rv, in_s.at[3]), pltpu.make_async_copy(back, bv, in_s.at[4])]
    for load in loads:
        load.start()
    extra = pltpu.make_async_copy(vf, sv, in_s.at[5])
    pl.when(late)(extra.start)
    answer = pltpu.make_async_copy(sl, solution_out, out_s.at[5])

    @pl.when(jnp.logical_not(late))
    def _():
        sl[...] = jnp.zeros_like(sl)
        answer.start()

    stores = []
    for j in range(STEPS):
        whole = pl.ds(j * NB, NB)
        loads[j].wait()
        so[whole] = yv[j].T
        stores.append(pltpu.make_async_copy(so.at[whole], solved_out.at[whole], out_s.at[j]))
        stores[-1].start()
    for k, (source, target) in enumerate(((rv, rest_out), (bv, back_out))):
        loads[3 + k].wait()
        stores.append(pltpu.make_async_copy(source, target, out_s.at[3 + k]))
        stores[-1].start()

    @pl.when(late)
    def _():
        extra.wait()
        sl[...] = sv[...].T
        answer.start()

    for store in stores:
        store.wait()
    answer.wait()


def local(factor, diag_inv, rhs, forward_values):
    anywhere = pl.BlockSpec(memory_space=pl.ANY)
    vmem = pl.BlockSpec(memory_space=pltpu.VMEM)
    dma = pltpu.SemaphoreType.DMA
    square = pltpu.VMEM((NB, NB), BF16)
    tall = pltpu.VMEM((NB, COLS), BF16)
    wide = pltpu.VMEM((COLS, NB), BF16)
    piece = pltpu.VMEM((PIECE, NB), F32)
    results = pl.pallas_call(
        kernel,
        name="solves",
        out_shape=(
            jax.ShapeDtypeStruct((STEPS, COLS, NB), BF16),
            jax.ShapeDtypeStruct((PIECE, NB), F32),
            jax.ShapeDtypeStruct((PIECE, NB), F32),
            jax.ShapeDtypeStruct((COLS, NB), F32),
        ),
        in_specs=[anywhere] * 4,
        out_specs=(anywhere, vmem, vmem, anywhere),
        scratch_shapes=[
            square, square, tall, tall, square, square, wide, wide,
            pltpu.VMEM((STEPS, COLS, NB), BF16),
            wide, wide, wide, wide,
            pltpu.VMEM((STEPS, PIECE, NB), BF16),
            wide,
            pltpu.VMEM((STEPS, PIECE, NB), BF16),
            wide,
            pltpu.VMEM((2, PIECE, NB), BF16),
            pltpu.VMEM((4, 2, 2, PIECE, NB), BF16),
            pltpu.VMEM((COLS, NB), F32),
            wide,
            pltpu.SemaphoreType.REGULAR((3,)), dma((4,)), dma((4,)),
            dma((4,)), dma((4,)), dma((3,)), dma((3, 4)), dma((3, 4)), dma((3,)), dma((3,)), dma((4,)), dma((2,)),
            dma((4,)), dma((4,)),
            dma(()), dma((4,)), dma(()), dma((3,)), dma((3,)), dma((3,)), dma(()), dma((4,)), dma((4,)),
            dma(()), dma((4,)), dma(()), dma(()), dma((4,)),
        ],
        compiler_params=pltpu.CompilerParams(
            collective_id=0, has_side_effects=True, vmem_limit_bytes=60 * 1024 * 1024
        ),
    )(factor, diag_inv, rhs, forward_values)
    solved, rest, back, answer = pl.pallas_call(
        hand_over,
        name="hand_over",
        out_shape=(
            jax.ShapeDtypeStruct((STEPS * NB, COLS), BF16),
            jax.ShapeDtypeStruct((PIECE, NB), F32),
            jax.ShapeDtypeStruct((PIECE, NB), F32),
            jax.ShapeDtypeStruct((NB, COLS), F32),
        ),
        in_specs=[anywhere] * 4,
        out_specs=(anywhere,) * 4,
        scratch_shapes=[
            pltpu.VMEM((STEPS, COLS, NB), BF16), pltpu.VMEM((STEPS * NB, COLS), BF16), piece, piece,
            pltpu.VMEM((COLS, NB), F32), pltpu.VMEM((NB, COLS), F32), dma((6,)), dma((6,)),
        ],
        compiler_params=pltpu.CompilerParams(vmem_limit_bytes=60 * 1024 * 1024),
    )(*results)
    return solved, rest.T, back.T, answer


def solution(mesh):
    placed = (P("row", "col"), P("row", None), P("row", None), P("row", None))
    return jax.shard_map(
        local,
        mesh=mesh,
        in_specs=placed,
        out_specs=(P(), P("row", "col"), P("col", "row"), P("row", None)),
        check_vma=False,
    )
```

time: 71.2 us -> 54 us (0.76)
  the two profiles are of different devices: /device:TPU:23 before, /device:TPU:32 now
where the time goes in v2:
time: 54 us; the launch traced here: 53.9 us
  Pallas kernels  53.2 us (99%)
  between operations  0.64 us (1%)
    pallas_call x1, Pallas kernels, local(): pl.pallas_call(kernel, name='solves', out_shape=(jax.ShapeDtypeStruct((ST...  50.3 us
    pallas_call x1, Pallas kernels, local(): pl.pallas_call(hand_over, name='hand_over', out_shape=(jax.ShapeDtypeStru...  2.89 us

profile of v2, /device:TPU:32, one launch (start us, length us, event | category | flops | bytes accessed | tf_op | source)
XLA Modules:
  0.0 53.9 jit_solution(9184604730486620046)
XLA Ops:
  0.6 50.3 %solves.1 = (bf16[3,256,1024]{2,1,0:T(8,128)(2,1)}, f32[16,1024]{1,0:T(8,128)}, f32[16,1024]{1,0:T(8,128)}, f32[256,1024]{1,0:T(8,128)}) custom-call(bf16[1024,1024]{1,0:T(8,128)(2,1)} %factor.1, bf16[1024,1024]{1,0:T(8,128)(2,1)} %inverse.1, bf16[1024,256]{1,0:T(8,128)(2,1)} %rhs.1, bf16[1024,256]{1,0:T(8,128)(2,1)} %start.1), custom_call_target="tpu_custom_call" | custom-call | tf_op jit(solution)/shard_map/solves/pallas_call | solution.py:617
  51.0 2.9 %hand_over.1 = (bf16[3072,256]{1,0:T(8,128)(2,1)}, f32[16,1024]{1,0:T(8,128)}, f32[16,1024]{1,0:T(8,128)}, f32[1024,256]{1,0:T(8,128)}) custom-call(bf16[3,256,1024]{2,1,0:T(8,128)(2,1)} %get-tuple-element.12.yt, f32[16,1024]{1,0:T(8,128)} %get-tuple-element.13.rest, f32[16,1024]{1,0:T(8,128)} %get-tuple-element.14.back, f32[256,1024]{1,0:T(8,128)} %get-tuple-element.15.vf), custom_call_target="tpu_custom_call" | custom-call | tf_op jit(solution)/shard_map/hand_over/pallas_call | solution.py:650

commit v3 on v2

--- a/solution.py
+++ b/solution.py
@@ -13,6 +13,7 @@
 PIECE = 16
 CHUNK = 64
 HALF = 512
+SIDE = (0, 0, 1)
 MESH = pl.DeviceIdType.MESH
 F32 = jnp.float32
 BF16 = jnp.bfloat16
@@ -34,10 +35,10 @@
     factor, inverse, rhs, start,
     solved_out, rest_out, back_out, solution_out,
     lv, dv, bv, uv, lt, dt, bt, ut,
-    yt, yc, pc, yr, pf, rp, qf, qr, qc, tb, wg, vf, vb,
+    yt, yc, pc, yr, pf, rp, qf, qr, qc, tb, wg, wl, vf, vb,
     ready, ld_s, out_s,
     yc_r, pc_r, own_r, s3_r, s4_r, rp_r, qr_r, qc_r, tb_r, ag_r, sib_r,
-    y0_s, s1_s, s1b_s, s2_s, s3_s, s4_s, pf_s, ch_s, pc_s, qf_s, qc_s, tb_s, ag_s, sib_s,
+    y0_s, s1_s, s1b_s, s2_s, s3_s, s4_s, pf_s, ch_s, pc_s, qf_s, qc_s, tb_s, w_s, ag_s, sib_s,
 ):
     r = lax.axis_index("row")
     c = lax.axis_index("col")
@@ -55,10 +56,7 @@
     row14 = r == 14
     row15 = r == 15
     late = r >= 13
-    first = jnp.where(e == 0, (x < 2) & (y < 2), ((x == 0) | (x == 3)) & ((y == 0) | (y == 3)))
     back1 = (r == 14) & (c == 13)
-    half = pl.multiple_of(e * HALF, HALF)
-    lanes = pl.ds(half, HALF)
     group = 2 * (x % 2) + y % 2
     mine = pl.ds(pl.multiple_of(group * CHUNK, CHUNK), CHUNK)
 
@@ -105,16 +103,16 @@
     def _():
         greet(1, 0)
 
-    pl.when(z == 1)(lambda: greet_other(1, 0))
-    pl.when(z == 2)(lambda: greet_other(2, 1))
     greet(r, c + 1 - 2 * e)
     loop(7, lambda k: greet(r, lax.rem(c + 2 + 2 * k, 16)))
     loop(8, lambda k: greet(lax.rem(r + 8, 16), 2 * k + e))
-    for col in range(STEPS):
-        pl.when(c != col)(lambda: greet(r, col))
+    pl.when((r == 1) & (c != 0))(lambda: greet(1, 0))
+    pl.when(c != 1)(lambda: greet(r, 1))
+    pl.when(c != 2)(lambda: greet(r, 2))
     pl.when(r != 13)(lambda: greet(13, c))
     pl.when(r != 14)(lambda: greet(14, c))
     pl.when(r != 15)(lambda: greet(15, c))
+
     def depth(j):
         return lax.rem(z - j + 8, 8)
 
@@ -122,23 +120,29 @@
         return yh * 8 + lax.rem(far + j, 8)
 
     def with_children(j, run):
-        for parent, children in ((0, (3, 1, 7)), (3, (5, 4, 2)), (7, (6,))):
+        for parent, children in ((0, (3, 7, 1)), (3, (4, 2)), (7, (6,)), (6, (5,))):
 
             @pl.when(depth(j) == parent)
             def _():
                 run(children)
 
     for j in range(STEPS):
-        with_children(j, lambda children: [greet(column(j, far), c) for far in children])
-
-    @pl.when(row14 & (c != 14))
+
+        @pl.when(e == SIDE[j])
+        def _():
+            with_children(j, lambda children: [greet(column(j, far), c) for far in children])
+
+    @pl.when(row14 & (c != 13))
+    def _():
+        greet(14, 13)
+
+    @pl.when(row13 & (c != 13))
+    def _():
+        greet(14, 13)
+
+    @pl.when(back1)
     def _():
         greet(15, 14)
-
-    @pl.when(row13 & (c != 13))
-    def _():
-        greet(15, 13)
-        greet(14, 13)
 
     pl.when(uses_d)(loads[0].wait)
     loads[1].wait()
@@ -182,16 +186,15 @@
 
     to_one = source_of((0, 2, 4, 12))
     to_two = source_of((6, 8, 13, 14))
-    count = 16 + jnp.where(c < STEPS, 15, 0) + jnp.where(z < STEPS, 2, 3) + jnp.where(late, 15, 0)
-    count = count + jnp.where(chain1 | chain2, 31, 0)
-    count = count + jnp.where(to_one | to_two | chain1, 1, 0)
-    count = count + jnp.where((row15 & ((c == 14) | (c == 13))) | back1, 15, 0)
+    count = 16 + jnp.where((c == 1) | (c == 2) | chain1, 15, 0) + jnp.where(late, 15, 0)
+    count = count + jnp.where(e == 0, jnp.where(z < 2, 1, 2), jnp.where(z == 2, 0, 1))
+    count = count + jnp.where(to_one | to_two | chain1 | (row15 & (c == 14)), 1, 0) + jnp.where(back1, 30, 0)
     pl.semaphore_wait(barrier, count)
 
     for j in range(STEPS):
-        near = jnp.where(depth(j) == 6, 7, jnp.where((depth(j) == 1) | (depth(j) == 3) | (depth(j) == 7), 0, 3))
-
-        @pl.when(depth(j) != 0)
+        near = jnp.where(depth(j) == 5, 6, jnp.where(depth(j) == 6, 7, jnp.where((depth(j) == 4) | (depth(j) == 2), 3, 0)))
+
+        @pl.when((e == SIDE[j]) & (depth(j) != 0))
         def _():
             pl.semaphore_signal(ready.at[j], inc=1, device_id=(column(j, near), c), device_id_type=MESH)
 
@@ -203,19 +206,13 @@
             def _():
                 remote(pf.at[rows(g, PIECE)], rp.at[c], pf_s, rp_r.at[c], r, g).start()
 
-    def scatter_qf(chunk):
+    def scatter_qf(chunk, wanted=lambda h: True):
         for k in range(4):
             h = 4 * chunk + k
 
-            @pl.when(h != r)
+            @pl.when((h != r) & wanted(h))
             def _():
                 remote(qf.at[rows(h, PIECE)], qr.at[r - 13], qf_s, qr_r.at[r - 13], h, c).start()
-
-    def send_t(slot, row):
-        def one(g):
-            remote(qf.at[rows(g, PIECE)], tb.at[slot], tb_s, tb_r.at[slot], row, g).start()
-
-        return one
 
     @pl.when(row0)
     def _():
@@ -233,80 +230,89 @@
                 part = pl.ds(chunk * CHUNK, CHUNK)
                 remote(yr.at[part], yc.at[part], y0_s, yc_r.at[chunk], 2, 0).start()
 
-        other = 3 - y
-        part = rows(2 * (x % 2) + other % 2, CHUNK)
-        remote(yr.at[part, lanes], yt.at[0, part, lanes], s1_s.at[0], own_r.at[0], 8, 4 * x + 2 * (other - 2) + e).start()
-        yt[0, mine, lanes] = yr[mine, lanes]
-
-    @pl.when(row15 & (c == 14))
-    def _():
+        @pl.when(e == SIDE[0])
+        def _():
+            other = 3 - y
+            part = rows(2 * (x % 2) + other % 2, CHUNK)
+            remote(yr.at[part], yt.at[0, part], s1_s.at[0], own_r.at[0, 0], 8, 4 * x + 2 * (other - 2) + e).start()
+            yt[0, mine] = yr[mine]
+
+    def send_back(target, recv):
         def one(step):
             chunk = lax.rem(5 - step, 4)
             part = rows(chunk, CHUNK)
-            remote(qf.at[part], qc.at[part], qc_s.at[chunk], qc_r.at[chunk], 14, 13).start()
+            remote(qf.at[part], target.at[part], qc_s.at[chunk], recv.at[chunk], 14, 13).start()
 
         loop(4, one)
-        for k in range(4):
-            sent(qf.at[pl.ds(0, CHUNK)], qc_s.at[k])
-        loop(16, send_t(0, 14))
-
-    @pl.when(row15 & (c == 13))
-    def _():
-        loop(16, send_t(0, 13))
+
+    pl.when(row15 & (c == 14))(lambda: send_back(qc, qc_r))
+    pl.when(row15 & (c == 13))(lambda: send_back(pc, pc_r))
 
     def scatter_s1(j, chunk):
         part = rows(chunk, CHUNK)
         a, b = chunk // 2, chunk % 2
+        if chunk == 0:
+            yt[j, part] = yr[part]
+            return
         for side in range(2):
             far = pl.ds(side * HALF, HALF)
             row = j + (8 * b if side else 0)
-            col = (12 * a + 2 * b + 1) if side else (4 * a + 2 * b)
-            own = (r == row) & (c == col)
-
-            @pl.when(jnp.logical_not(own))
-            def _():
-                remote(yr.at[part, far], yt.at[j, part, far], s1_s.at[chunk], own_r.at[j], row, col).start()
-
-            @pl.when(own)
-            def _():
-                yt[j, part, far] = yr[part, far]
-
-    def spread(step):
-        j = jnp.where(z == 1, (1, 0, 2)[step], jnp.where(z == 2, (2, 0, 1)[step], step))
-        block = yt.at[j, mine, lanes]
+            col = (12 * a if side else 4 * a) + 2 * b + SIDE[j]
+            remote(yr.at[part, far], yt.at[j, part, far], s1_s.at[chunk], own_r.at[j, side], row, col).start()
+
+    halves = (pl.ds(0, HALF), pl.ds(HALF, HALF))
+    heads = ((x < 2) & (y < 2), ((x == 0) | (x == 3)) & ((y == 0) | (y == 3)))
+
+    def spread(j):
+        block = yt.at[j, mine]
+        parts = [yt.at[j, mine, side] for side in halves]
         local = (row0 & (j == 0)) | (chain1 & (j == 1)) | (chain2 & (j == 2))
-
-        @pl.when(jnp.logical_not(local))
-        def _():
-            got(block, own_r.at[j])
-
-        def to_chip(send, recv, tx, ty):
-            remote(block, block, send, recv, 8 * (ty // 2) + z, 4 * tx + 2 * (ty % 2) + e).start()
-
-        @pl.when((z == j) & (j > 0) & first)
-        def _():
-            x2, y2 = lax.rem(x + 2, 4), lax.rem(y + 2, 4)
-            to_chip(s1b_s, own_r.at[j], x2, y2)
-            to_chip(s1b_s, own_r.at[j], x2, y)
-            to_chip(s1b_s, own_r.at[j], x, y2)
-
-        x1, y1 = lax.rem(x + 1 + 2 * e, 4), lax.rem(y + 1 + 2 * e, 4)
-        to_chip(s3_s.at[j], s3_r.at[j, group], x1, y1)
-        to_chip(s3_s.at[j], s3_r.at[j, group], x1, y)
-        to_chip(s3_s.at[j], s3_r.at[j, group], x, y1)
+        starts = (z == j) & (j > 0)
+
+        def to_chip(part, send, recv, tx, ty):
+            remote(part, part, send, recv, 8 * (ty // 2) + z, 4 * tx + 2 * (ty % 2) + e).start()
+
+        for k in range(2):
+
+            @pl.when(starts & heads[k])
+            def _():
+                @pl.when(jnp.logical_not(local))
+                def _():
+                    got(parts[k], own_r.at[j, k])
+
+                x2, y2 = lax.rem(x + 2, 4), lax.rem(y + 2, 4)
+                to_chip(parts[k], s1b_s.at[k], own_r.at[j, k], x2, y2)
+                to_chip(parts[k], s1b_s.at[k], own_r.at[j, k], x2, y)
+                to_chip(parts[k], s1b_s.at[k], own_r.at[j, k], x, y2)
+
+        for k in range(2):
+
+            @pl.when(starts & jnp.logical_not(heads[k]))
+            def _():
+                got(parts[k], own_r.at[j, k])
+
+        @pl.when(jnp.logical_not(starts | local))
+        def _():
+            got(block, own_r.at[j, 0])
+
+        for k in range(2):
+            x1, y1 = lax.rem(x + 1 + 2 * k, 4), lax.rem(y + 1 + 2 * k, 4)
+            to_chip(parts[k], s3_s.at[j], s3_r.at[j, group], x1, y1)
+            to_chip(parts[k], s3_s.at[j], s3_r.at[j, group], x1, y)
+            to_chip(parts[k], s3_s.at[j], s3_r.at[j, group], x, y1)
         remote(block, block, s4_s.at[j], s4_r.at[j, group], r, c + 1 - 2 * e).start()
 
         def run(children):
             pl.semaphore_wait(ready.at[j], len(children))
             for far in children:
-                remote(block, block, s2_s.at[j], own_r.at[j], column(j, far), c).start()
+                remote(block, block, s2_s.at[j], own_r.at[j, 0], column(j, far), c).start()
 
         with_children(j, run)
 
     def collect(j):
         def one(step):
             chunk = 3 - step
-            block = yt.at[j, rows(chunk, CHUNK), lanes]
+            block = yt.at[j, rows(chunk, CHUNK)]
 
             @pl.when(chunk != group)
             def _():
@@ -316,12 +322,13 @@
         loop(4, one)
 
     def apply(j):
-        other = pl.ds(pl.multiple_of(HALF - half, HALF), HALF)
-
         def one(step):
             chunk = 3 - step
             part = rows(chunk, CHUNK)
-            got(yt.at[j, part, other], s4_r.at[j, chunk])
+
+            @pl.when(e != SIDE[j])
+            def _():
+                got(yt.at[j, part], s4_r.at[j, chunk])
 
             @pl.when((c == j) & (r >= 3))
             def _():
@@ -339,21 +346,19 @@
         pltpu.make_async_copy(yt.at[j], solved_out.at[j], out_s.at[j]).start()
 
     def centre():
+        block = wg.at[x, yl, e]
+
+        @pl.when(row13)
+        def _():
+            got(tb, tb_r.at[0])
+            block[...] = (ut[rows(c, PIECE)].astype(F32) - tb[...].astype(F32)).astype(BF16)
+
+        @pl.when(row14 & (c != 13))
+        def _():
+            got(block, tb_r.at[0])
+
         @pl.when(row14 | row13)
         def _():
-            got(tb.at[0], tb_r.at[0])
-
-            @pl.when(row13)
-            def _():
-                got(tb.at[1], tb_r.at[1])
-
-            total = tb[0].astype(F32)
-            total = total + jnp.where(row13, tb[1].astype(F32), 0.0)
-            summed = total.astype(BF16).astype(F32)
-            piece = (ut[rows(c, PIECE)].astype(F32) - summed).astype(BF16)
-            wg[x, yl, e] = piece
-            block = wg.at[x, yl, e]
-
             def one(k):
                 to = lax.rem(2 * x + yl + 1 + k, 8)
                 remote(block, block, ag_s, ag_r.at[x], r, 2 * to + e).start()
@@ -451,75 +456,108 @@
             part = rows(chunk, CHUNK)
             got(qc.at[part], qc_r.at[chunk])
             centred = (ut[part].astype(F32) - qc[part].astype(F32)).astype(BF16)
+            wl[part] = centred
             answer = product(centred, dv[...]).astype(BF16)
-            qf[part] = product(answer, lv[...]).astype(BF16)
+            partial = product(answer, lv[...]).astype(BF16)
+            qf[part] = partial
+            got(pc.at[part], pc_r.at[chunk])
+            yc[part] = (pc[part].astype(F32) + partial.astype(F32)).astype(BF16)
             for k in range(4):
-                send_t(1, 13)(4 * chunk + k)
+                g = 4 * chunk + k
+                remote(yc.at[rows(g, PIECE)], tb, tb_s, tb_r.at[0], 13, g).start()
+            for k in range(4):
+                piece = rows(4 * chunk + k, PIECE)
+                target = wg.at[chunk, k // 2, k % 2]
+
+                @pl.when(4 * chunk + k != c)
+                def _():
+                    remote(wl.at[piece], target, w_s, tb_r.at[0], 14, 4 * chunk + k).start()
+
+                @pl.when(4 * chunk + k == c)
+                def _():
+                    target[...] = wl[piece]
 
         loop(4, one)
 
-    spread(0)
+    middle = row13 | row14
+    first_two = (jnp.where(z == 1, 1, 0), jnp.where(e == 1, 2, jnp.where(z == 1, 0, 1)))
+
+    def below(h):
+        return (h % 8 >= 4) & (h % 8 < 7)
+
+    @pl.when((e == 0) & jnp.logical_not(row13))
+    def _():
+        spread(first_two[0])
 
     @pl.when(row15 & (c < 15))
     def _():
-        loop(4, scatter_qf)
-
-    spread(1)
+        loop(4, lambda chunk: scatter_qf(chunk, lambda h: jnp.logical_not(below(h))))
+
     centre()
-    collect(0)
-    apply(0)
+
+    @pl.when(jnp.logical_not(middle))
+    def _():
+        spread(first_two[1])
+
+    @pl.when(row15 & (c < 15))
+    def _():
+        loop(4, lambda chunk: scatter_qf(chunk, below))
+
+    @pl.when((e == 0) & jnp.logical_not(middle))
+    def _():
+        collect(0)
+        apply(0)
+
     gather()
-    spread(2)
+
+    @pl.when(row13)
+    def _():
+        pl.when(e == 0)(lambda: spread(0))
+        spread(first_two[1])
+
     solve()
 
+    @pl.when(row14)
+    def _():
+        spread(first_two[1])
+
+    @pl.when((e == 0) & middle)
+    def _():
+        collect(0)
+        apply(0)
+
     @pl.when(chain1 | chain2)
     def _():
         loop(4, scatter_pf)
 
-    collect(1)
-    apply(1)
-    collect(2)
+    @pl.when(e == 0)
+    def _():
+        collect(1)
+        apply(1)
+
+    @pl.when(e == 1)
+    def _():
+        collect(2)
+        apply(0)
+        apply(1)
+
     done = pltpu.make_async_copy(vf, solution_out, out_s.at[3])
     pl.when(late)(done.start)
     apply(2)
 
-    rest_out[...] = bt[rows(c, PIECE)].astype(F32)
     for j in range(STEPS):
 
-        @pl.when((r == 1) if j == 0 else (r > j))
-        def _():
-            @pl.when(c == j)
-            def _():
-                rest_out[...] -= pf[rows(c, PIECE)].astype(F32)
-
-            @pl.when(c != j)
-            def _():
-                got(rp.at[j], rp_r.at[j])
-                rest_out[...] -= rp[j].astype(F32)
-
-    back_out[...] = jnp.zeros_like(back_out)
-    for j in range(STEPS):
-
-        @pl.when(c < 13 + j)
-        def _():
-            @pl.when(r == 13 + j)
-            def _():
-                back_out[...] += qf[rows(r, PIECE)].astype(F32)
-
-            @pl.when(r != 13 + j)
-            def _():
-                got(qr.at[j], qr_r.at[j])
-                back_out[...] += qr[j].astype(F32)
-
-    side = pl.ds(0, HALF)
-    for j in range(STEPS):
-        sent(yt.at[j, pl.ds(0, 192), side], s3_s.at[j])
-        sent(yt.at[j, :, side], s4_s.at[j])
-        with_children(j, lambda children: sent(yt.at[j, pl.ds(0, len(children) * CHUNK), side], s2_s.at[j]))
-
-    @pl.when(((z == 1) | (z == 2)) & first)
-    def _():
-        sent(yt.at[0, pl.ds(0, 192), side], s1b_s)
+        @pl.when(e == SIDE[j])
+        def _():
+            sent(yt.at[j, pl.ds(0, 192)], s3_s.at[j])
+            sent(yt.at[j], s4_s.at[j])
+            with_children(j, lambda children: sent(yt.at[j, pl.ds(0, len(children) * CHUNK)], s2_s.at[j]))
+
+    for k in range(2):
+
+        @pl.when(((z == 1) & (e == 0) | (z == 2) & (e == 1)) & heads[k])
+        def _():
+            sent(yt.at[0, pl.ds(0, 192), halves[k]], s1b_s.at[k])
 
     @pl.when(row0)
     def _():
@@ -527,13 +565,14 @@
         def _():
             sent(yr.at[pl.ds(0, CHUNK)], y0_s)
 
-        sent(yr.at[pl.ds(0, CHUNK), side], s1_s.at[0])
+        @pl.when(e == SIDE[0])
+        def _():
+            sent(yr.at[pl.ds(0, CHUNK)], s1_s.at[0])
 
     @pl.when(chain1 | chain2)
     def _():
-        sent(yr.at[pl.ds(0, CHUNK), side], s1_s.at[0])
         for k in range(1, 4):
-            sent(yr.at[pl.ds(0, 2 * CHUNK), side], s1_s.at[k])
+            sent(yr.at[pl.ds(0, CHUNK)], s1_s.at[k])
 
     @pl.when(chain1)
     def _():
@@ -553,15 +592,52 @@
     def _():
         sent(qf.at[pl.ds(0, 240)], qf_s)
 
-    @pl.when((row15 & ((c == 14) | (c == 13))) | back1)
+    @pl.when(row15 & ((c == 13) | (c == 14)))
+    def _():
+        for k in range(4):
+            sent(qf.at[pl.ds(0, CHUNK)], qc_s.at[k])
+
+    @pl.when(back1)
     def _():
         sent(qf, tb_s)
+
+    @pl.when(back1)
+    def _():
+        sent(qf.at[pl.ds(0, 240)], w_s)
 
     @pl.when(row14 | row13)
     def _():
         sent(qf.at[pl.ds(0, 112)], ag_s)
         for k in range(4):
             sent(wg.at[0, :, 0], sib_s.at[k])
+
+    rest_out[...] = bt[rows(c, PIECE)].astype(F32)
+    for j in range(STEPS):
+
+        @pl.when((r == 1) if j == 0 else (r > j))
+        def _():
+            @pl.when(c == j)
+            def _():
+                rest_out[...] -= pf[rows(c, PIECE)].astype(F32)
+
+            @pl.when(c != j)
+            def _():
+                got(rp.at[j], rp_r.at[j])
+                rest_out[...] -= rp[j].astype(F32)
+
+    back_out[...] = jnp.zeros_like(back_out)
+    for j in range(STEPS):
+
+        @pl.when(c < 13 + j)
+        def _():
+            @pl.when(r == 13 + j)
+            def _():
+                back_out[...] += qf[rows(r, PIECE)].astype(F32)
+
+            @pl.when(r != 13 + j)
+            def _():
+                got(qr.at[j], qr_r.at[j])
+                back_out[...] += qr[j].astype(F32)
 
     for j in range(STEPS):
         pltpu.make_async_copy(yt.at[j], solved_out.at[j], out_s.at[j]).wait()
@@ -633,15 +709,16 @@
             wide,
             pltpu.VMEM((STEPS, PIECE, NB), BF16),
             wide,
-            pltpu.VMEM((2, PIECE, NB), BF16),
+            pltpu.VMEM((PIECE, NB), BF16),
             pltpu.VMEM((4, 2, 2, PIECE, NB), BF16),
+            wide,
             pltpu.VMEM((COLS, NB), F32),
             wide,
             pltpu.SemaphoreType.REGULAR((3,)), dma((4,)), dma((4,)),
-            dma((4,)), dma((4,)), dma((3,)), dma((3, 4)), dma((3, 4)), dma((3,)), dma((3,)), dma((4,)), dma((2,)),
+            dma((4,)), dma((4,)), dma((3, 2)), dma((3, 4)), dma((3, 4)), dma((3,)), dma((3,)), dma((4,)), dma((2,)),
             dma((4,)), dma((4,)),
-            dma(()), dma((4,)), dma(()), dma((3,)), dma((3,)), dma((3,)), dma(()), dma((4,)), dma((4,)),
-            dma(()), dma((4,)), dma(()), dma(()), dma((4,)),
+            dma(()), dma((4,)), dma((2,)), dma((3,)), dma((3,)), dma((3,)), dma(()), dma((4,)), dma((4,)),
+            dma(()), dma((4,)), dma(()), dma(()), dma(()), dma((4,)),
         ],
         compiler_params=pltpu.CompilerParams(
             collective_id=0, has_side_effects=True, vmem_limit_bytes=60 * 1024 * 1024

time: 54 us -> 49.3 us (0.913)
  the two profiles are of different devices: /device:TPU:32 before, /device:TPU:57 now
where the time goes in v3:
time: 49.3 us; the launch traced here: 49.2 us
  Pallas kernels  48.6 us (99%)
  between operations  0.64 us (1%)
    pallas_call x1, Pallas kernels, local(): pl.pallas_call(kernel, name='solves', out_shape=(jax.ShapeDtypeStruct((ST...  45.7 us
    pallas_call x1, Pallas kernels, local(): pl.pallas_call(hand_over, name='hand_over', out_shape=(jax.ShapeDtypeStru...  2.89 us

profile of v3, /device:TPU:57, one launch (start us, length us, event | category | flops | bytes accessed | tf_op | source)
XLA Modules:
  0.0 49.2 jit_solution(12571831621395166572)
XLA Ops:
  0.6 45.7 %solves.1 = (bf16[3,256,1024]{2,1,0:T(8,128)(2,1)}, f32[16,1024]{1,0:T(8,128)}, f32[16,1024]{1,0:T(8,128)}, f32[256,1024]{1,0:T(8,128)}) custom-call(bf16[1024,1024]{1,0:T(8,128)(2,1)} %factor.1, bf16[1024,1024]{1,0:T(8,128)(2,1)} %inverse.1, bf16[1024,256]{1,0:T(8,128)(2,1)} %rhs.1, bf16[1024,256]{1,0:T(8,128)(2,1)} %start.1), custom_call_target="tpu_custom_call" | custom-call | tf_op jit(solution)/shard_map/solves/pallas_call | solution.py:693
  46.3 2.9 %hand_over.1 = (bf16[3072,256]{1,0:T(8,128)(2,1)}, f32[16,1024]{1,0:T(8,128)}, f32[16,1024]{1,0:T(8,128)}, f32[1024,256]{1,0:T(8,128)}) custom-call(bf16[3,256,1024]{2,1,0:T(8,128)(2,1)} %get-tuple-element.12.yt, f32[16,1024]{1,0:T(8,128)} %get-tuple-element.13.rest, f32[16,1024]{1,0:T(8,128)} %get-tuple-element.14.back, f32[256,1024]{1,0:T(8,128)} %get-tuple-element.15.vf), custom_call_target="tpu_custom_call" | custom-call | tf_op jit(solution)/shard_map/hand_over/pallas_call | solution.py:727

commit v4 on v3

--- a/solution.py
+++ b/solution.py
@@ -33,10 +33,10 @@
 
 def kernel(
     factor, inverse, rhs, start,
-    solved_out, rest_out, back_out, solution_out,
+    yt, rest_out, back_out, vf,
     lv, dv, bv, uv, lt, dt, bt, ut,
-    yt, yc, pc, yr, pf, rp, qf, qr, qc, tb, wg, wl, vf, vb,
-    ready, ld_s, out_s,
+    yc, pc, yr, pf, rp, qf, qr, qc, tb, wg, wl, vb,
+    ready, ld_s,
     yc_r, pc_r, own_r, s3_r, s4_r, rp_r, qr_r, qc_r, tb_r, ag_r, sib_r,
     y0_s, s1_s, s1b_s, s2_s, s3_s, s4_s, pf_s, ch_s, pc_s, qf_s, qc_s, tb_s, w_s, ag_s, sib_s,
 ):
@@ -58,6 +58,7 @@
     late = r >= 13
     back1 = (r == 14) & (c == 13)
     group = 2 * (x % 2) + y % 2
+    halves = (pl.ds(0, HALF), pl.ds(HALF, HALF))
     mine = pl.ds(pl.multiple_of(group * CHUNK, CHUNK), CHUNK)
 
     def remote(src, dst, send, recv, row, col):
@@ -120,7 +121,7 @@
         return yh * 8 + lax.rem(far + j, 8)
 
     def with_children(j, run):
-        for parent, children in ((0, (3, 7, 1)), (3, (4, 2)), (7, (6,)), (6, (5,))):
+        for parent, children in ((0, (2, 7, 1)), (2, (4, 3)), (7, (6,)), (6, (5,))):
 
             @pl.when(depth(j) == parent)
             def _():
@@ -145,15 +146,12 @@
         greet(15, 14)
 
     pl.when(uses_d)(loads[0].wait)
-    loads[1].wait()
 
     @pl.when(row0)
     def _():
+        loads[1].wait()
         value = jnp.dot(dv[...], bv[...], preferred_element_type=F32)
         yr[...] = value.astype(BF16).T
-
-    bt[...] = bv[...].T
-    pl.when(uses_l)(loads[2].wait)
 
     @pl.when(late)
     def _():
@@ -166,9 +164,7 @@
         vf[...] = value
         vb[...] = value.astype(BF16)
 
-        @pl.when(c < 15)
-        def _():
-            qf[...] = product(vb[...], lv[...]).astype(BF16)
+    pl.when(uses_l)(loads[2].wait)
 
     @pl.when(chain1 | chain2)
     def _():
@@ -192,7 +188,7 @@
     pl.semaphore_wait(barrier, count)
 
     for j in range(STEPS):
-        near = jnp.where(depth(j) == 5, 6, jnp.where(depth(j) == 6, 7, jnp.where((depth(j) == 4) | (depth(j) == 2), 3, 0)))
+        near = jnp.where(depth(j) == 5, 6, jnp.where(depth(j) == 6, 7, jnp.where((depth(j) == 4) | (depth(j) == 3), 2, 0)))
 
         @pl.when((e == SIDE[j]) & (depth(j) != 0))
         def _():
@@ -234,19 +230,30 @@
         def _():
             other = 3 - y
             part = rows(2 * (x % 2) + other % 2, CHUNK)
-            remote(yr.at[part], yt.at[0, part], s1_s.at[0], own_r.at[0, 0], 8, 4 * x + 2 * (other - 2) + e).start()
+            for k, side in enumerate(halves):
+                to = (8, 4 * x + 2 * (other - 2) + e)
+                remote(yr.at[part, side], yt.at[0, part, side], s1_s.at[0], own_r.at[0, k], *to).start()
             yt[0, mine] = yr[mine]
 
-    def send_back(target, recv):
+    @pl.when(row15 & (c < 15))
+    def _():
         def one(step):
-            chunk = lax.rem(5 - step, 4)
+            chunk = lax.rem(6 - step, 4)
             part = rows(chunk, CHUNK)
-            remote(qf.at[part], target.at[part], qc_s.at[chunk], recv.at[chunk], 14, 13).start()
+            qf[part] = product(vb[part], lv[...]).astype(BF16)
+            for col, target, recv in ((14, qc, qc_r), (13, pc, pc_r)):
+
+                @pl.when(c == col)
+                def _():
+                    remote(qf.at[part], target.at[part], qc_s.at[chunk], recv.at[chunk], 14, 13).start()
 
         loop(4, one)
 
-    pl.when(row15 & (c == 14))(lambda: send_back(qc, qc_r))
-    pl.when(row15 & (c == 13))(lambda: send_back(pc, pc_r))
+    @pl.when(jnp.logical_not(row0))
+    def _():
+        loads[1].wait()
+
+    bt[...] = bv[...].T
 
     def scatter_s1(j, chunk):
         part = rows(chunk, CHUNK)
@@ -260,54 +267,45 @@
             col = (12 * a if side else 4 * a) + 2 * b + SIDE[j]
             remote(yr.at[part, far], yt.at[j, part, far], s1_s.at[chunk], own_r.at[j, side], row, col).start()
 
-    halves = (pl.ds(0, HALF), pl.ds(HALF, HALF))
     heads = ((x < 2) & (y < 2), ((x == 0) | (x == 3)) & ((y == 0) | (y == 3)))
 
     def spread(j):
-        block = yt.at[j, mine]
-        parts = [yt.at[j, mine, side] for side in halves]
         local = (row0 & (j == 0)) | (chain1 & (j == 1)) | (chain2 & (j == 2))
         starts = (z == j) & (j > 0)
-
-        def to_chip(part, send, recv, tx, ty):
-            remote(part, part, send, recv, 8 * (ty // 2) + z, 4 * tx + 2 * (ty % 2) + e).start()
-
-        for k in range(2):
-
-            @pl.when(starts & heads[k])
-            def _():
-                @pl.when(jnp.logical_not(local))
-                def _():
-                    got(parts[k], own_r.at[j, k])
-
+        turned = starts & heads[1] & jnp.logical_not(heads[0])
+
+        for step in range(2):
+            side = jnp.where(turned, 1 - step, step)
+            part = yt.at[j, mine, pl.ds(pl.multiple_of(side * HALF, HALF), HALF)]
+
+            def to_chip(send, recv, tx, ty):
+                remote(part, part, send, recv, 8 * (ty // 2) + z, 4 * tx + 2 * (ty % 2) + e).start()
+
+            @pl.when(jnp.logical_not(local))
+            def _():
+                got(part, own_r.at[j, side])
+
+            @pl.when(starts & jnp.where(side == 0, heads[0], heads[1]))
+            def _():
                 x2, y2 = lax.rem(x + 2, 4), lax.rem(y + 2, 4)
-                to_chip(parts[k], s1b_s.at[k], own_r.at[j, k], x2, y2)
-                to_chip(parts[k], s1b_s.at[k], own_r.at[j, k], x2, y)
-                to_chip(parts[k], s1b_s.at[k], own_r.at[j, k], x, y2)
-
-        for k in range(2):
-
-            @pl.when(starts & jnp.logical_not(heads[k]))
-            def _():
-                got(parts[k], own_r.at[j, k])
-
-        @pl.when(jnp.logical_not(starts | local))
-        def _():
-            got(block, own_r.at[j, 0])
-
-        for k in range(2):
-            x1, y1 = lax.rem(x + 1 + 2 * k, 4), lax.rem(y + 1 + 2 * k, 4)
-            to_chip(parts[k], s3_s.at[j], s3_r.at[j, group], x1, y1)
-            to_chip(parts[k], s3_s.at[j], s3_r.at[j, group], x1, y)
-            to_chip(parts[k], s3_s.at[j], s3_r.at[j, group], x, y1)
+                to_chip(s1b_s.at[side], own_r.at[j, side], x2, y2)
+                to_chip(s1b_s.at[side], own_r.at[j, side], x2, y)
+                to_chip(s1b_s.at[side], own_r.at[j, side], x, y2)
+
+            def run(children):
+                if step == 0:
+                    pl.semaphore_wait(ready.at[j], len(children))
+                for far in children:
+                    remote(part, part, s2_s.at[j], own_r.at[j, side], column(j, far), c).start()
+
+            with_children(j, run)
+            x1, y1 = lax.rem(x + 1 + 2 * side, 4), lax.rem(y + 1 + 2 * side, 4)
+            to_chip(s3_s.at[j], s3_r.at[j, group], x1, y1)
+            to_chip(s3_s.at[j], s3_r.at[j, group], x1, y)
+            to_chip(s3_s.at[j], s3_r.at[j, group], x, y1)
+
+        block = yt.at[j, mine]
         remote(block, block, s4_s.at[j], s4_r.at[j, group], r, c + 1 - 2 * e).start()
-
-        def run(children):
-            pl.semaphore_wait(ready.at[j], len(children))
-            for far in children:
-                remote(block, block, s2_s.at[j], own_r.at[j, 0], column(j, far), c).start()
-
-        with_children(j, run)
 
     def collect(j):
         def one(step):
@@ -343,7 +341,6 @@
                     scatter_pf(chunk)
 
         loop(4, one)
-        pltpu.make_async_copy(yt.at[j], solved_out.at[j], out_s.at[j]).start()
 
     def centre():
         block = wg.at[x, yl, e]
@@ -369,7 +366,7 @@
         @pl.when(row14 | row13)
         def _():
             def one(step):
-                chunk = lax.rem(5 - step, 4)
+                chunk = lax.rem(6 - step, 4)
 
                 @pl.when(chunk == x)
                 def _():
@@ -388,7 +385,7 @@
         @pl.when(row14 | row13)
         def _():
             def one(step):
-                chunk = lax.rem(5 - step, 4)
+                chunk = lax.rem(6 - step, 4)
                 part = rows(chunk, CHUNK)
                 got(wg.at[chunk, :, 1 - e], sib_r.at[chunk])
                 answer = product(wg[chunk].reshape(CHUNK, NB), dv[...])
@@ -452,7 +449,7 @@
     @pl.when(back1)
     def _():
         def one(step):
-            chunk = lax.rem(5 - step, 4)
+            chunk = lax.rem(6 - step, 4)
             part = rows(chunk, CHUNK)
             got(qc.at[part], qc_r.at[chunk])
             centred = (ut[part].astype(F32) - qc[part].astype(F32)).astype(BF16)
@@ -510,14 +507,13 @@
 
     gather()
 
-    @pl.when(row13)
-    def _():
-        pl.when(e == 0)(lambda: spread(0))
-        spread(first_two[1])
+    @pl.when((e == 0) & row13)
+    def _():
+        spread(0)
 
     solve()
 
-    @pl.when(row14)
+    @pl.when(middle)
     def _():
         spread(first_two[1])
 
@@ -541,8 +537,6 @@
         apply(0)
         apply(1)
 
-    done = pltpu.make_async_copy(vf, solution_out, out_s.at[3])
-    pl.when(late)(done.start)
     apply(2)
 
     for j in range(STEPS):
@@ -639,44 +633,28 @@
                 got(qr.at[j], qr_r.at[j])
                 back_out[...] += qr[j].astype(F32)
 
-    for j in range(STEPS):
-        pltpu.make_async_copy(yt.at[j], solved_out.at[j], out_s.at[j]).wait()
-    pl.when(late)(done.wait)
-
-
-def hand_over(yt, rest, back, vf, solved_out, rest_out, back_out, solution_out, yv, so, rv, bv, sv, sl, in_s, out_s):
+
+def hand_over(yt, rest, back, vf, solved_out, rest_out, back_out, solution_out, so, sl, sems):
     late = lax.axis_index("row") >= 13
-    loads = [pltpu.make_async_copy(yt.at[j], yv.at[j], in_s.at[j]) for j in range(STEPS)]
-    loads += [pltpu.make_async_copy(rest, rv, in_s.at[3]), pltpu.make_async_copy(back, bv, in_s.at[4])]
-    for load in loads:
-        load.start()
-    extra = pltpu.make_async_copy(vf, sv, in_s.at[5])
-    pl.when(late)(extra.start)
-    answer = pltpu.make_async_copy(sl, solution_out, out_s.at[5])
+    answer = pltpu.make_async_copy(sl, solution_out, sems.at[5])
+    stores = [pltpu.make_async_copy(rest, rest_out, sems.at[3]), pltpu.make_async_copy(back, back_out, sems.at[4])]
+    for store in stores:
+        store.start()
 
     @pl.when(jnp.logical_not(late))
     def _():
         sl[...] = jnp.zeros_like(sl)
-        answer.start()
-
-    stores = []
+
+    @pl.when(late)
+    def _():
+        sl[...] = vf[...].T
+
+    answer.start()
     for j in range(STEPS):
         whole = pl.ds(j * NB, NB)
-        loads[j].wait()
-        so[whole] = yv[j].T
-        stores.append(pltpu.make_async_copy(so.at[whole], solved_out.at[whole], out_s.at[j]))
+        so[whole] = yt[j].T
+        stores.append(pltpu.make_async_copy(so.at[whole], solved_out.at[whole], sems.at[j]))
         stores[-1].start()
-    for k, (source, target) in enumerate(((rv, rest_out), (bv, back_out))):
-        loads[3 + k].wait()
-        stores.append(pltpu.make_async_copy(source, target, out_s.at[3 + k]))
-        stores[-1].start()
-
-    @pl.when(late)
-    def _():
-        extra.wait()
-        sl[...] = sv[...].T
-        answer.start()
-
     for store in stores:
         store.wait()
     answer.wait()
@@ -689,21 +667,19 @@
     square = pltpu.VMEM((NB, NB), BF16)
     tall = pltpu.VMEM((NB, COLS), BF16)
     wide = pltpu.VMEM((COLS, NB), BF16)
-    piece = pltpu.VMEM((PIECE, NB), F32)
     results = pl.pallas_call(
         kernel,
         name="solves",
         out_shape=(
-            jax.ShapeDtypeStruct((STEPS, COLS, NB), BF16),
-            jax.ShapeDtypeStruct((PIECE, NB), F32),
-            jax.ShapeDtypeStruct((PIECE, NB), F32),
-            jax.ShapeDtypeStruct((COLS, NB), F32),
+            pltpu.VMEM((STEPS, COLS, NB), BF16),
+            pltpu.VMEM((PIECE, NB), F32),
+            pltpu.VMEM((PIECE, NB), F32),
+            pltpu.VMEM((COLS, NB), F32),
         ),
         in_specs=[anywhere] * 4,
-        out_specs=(anywhere, vmem, vmem, anywhere),
+        out_specs=(vmem,) * 4,
         scratch_shapes=[
             square, square, tall, tall, square, square, wide, wide,
-            pltpu.VMEM((STEPS, COLS, NB), BF16),
             wide, wide, wide, wide,
             pltpu.VMEM((STEPS, PIECE, NB), BF16),
             wide,
@@ -712,9 +688,8 @@
             pltpu.VMEM((PIECE, NB), BF16),
             pltpu.VMEM((4, 2, 2, PIECE, NB), BF16),
             wide,
-            pltpu.VMEM((COLS, NB), F32),
             wide,
-            pltpu.SemaphoreType.REGULAR((3,)), dma((4,)), dma((4,)),
+            pltpu.SemaphoreType.REGULAR((3,)), dma((4,)),
             dma((4,)), dma((4,)), dma((3, 2)), dma((3, 4)), dma((3, 4)), dma((3,)), dma((3,)), dma((4,)), dma((2,)),
             dma((4,)), dma((4,)),
             dma(()), dma((4,)), dma((2,)), dma((3,)), dma((3,)), dma((3,)), dma(()), dma((4,)), dma((4,)),
@@ -733,13 +708,10 @@
             jax.ShapeDtypeStruct((PIECE, NB), F32),
             jax.ShapeDtypeStruct((NB, COLS), F32),
         ),
-        in_specs=[anywhere] * 4,
+        in_specs=[vmem] * 4,
         out_specs=(anywhere,) * 4,
-        scratch_shapes=[
-            pltpu.VMEM((STEPS, COLS, NB), BF16), pltpu.VMEM((STEPS * NB, COLS), BF16), piece, piece,
-            pltpu.VMEM((COLS, NB), F32), pltpu.VMEM((NB, COLS), F32), dma((6,)), dma((6,)),
-        ],
-        compiler_params=pltpu.CompilerParams(vmem_limit_bytes=60 * 1024 * 1024),
+        scratch_shapes=[pltpu.VMEM((STEPS * NB, COLS), BF16), pltpu.VMEM((NB, COLS), F32), dma((6,))],
+        compiler_params=pltpu.CompilerParams(vmem_limit_bytes=32 * 1024 * 1024),
     )(*results)
     return solved, rest.T, back.T, answer
 

time: 49.3 us -> 45.5 us (0.923)
  the two profiles are of different devices: /device:TPU:57 before, /device:TPU:36 now
where the time goes in v4:
time: 45.5 us; the launch traced here: 45.4 us
  Pallas kernels  44.7 us (98%)
  between operations  0.64 us (1%)
    pallas_call x1, Pallas kernels, local(): pl.pallas_call(kernel, name='solves', out_shape=(pltpu.VMEM((STEPS, COLS,...  43.1 us
    pallas_call x1, Pallas kernels, local(): pl.pallas_call(hand_over, name='hand_over', out_shape=(jax.ShapeDtypeStru...  1.62 us

profile of v4, /device:TPU:36, one launch (start us, length us, event | category | flops | bytes accessed | tf_op | source)
XLA Modules:
  0.0 45.4 jit_solution(10074935139387043933)
XLA Ops:
  0.6 43.1 %solves.1 = (bf16[3,256,1024]{2,1,0:T(8,128)(2,1)S(1)}, f32[16,1024]{1,0:T(8,128)S(1)}, f32[16,1024]{1,0:T(8,128)S(1)}, f32[256,1024]{1,0:T(8,128)S(1)}) custom-call(bf16[1024,1024]{1,0:T(8,128)(2,1)} %factor.1, bf16[1024,1024]{1,0:T(8,128)(2,1)} %inverse.1, bf16[1024,256]{1,0:T(8,128)(2,1)} %rhs.1, bf16[1024,256]{1,0:T(8,128)(2,1)} %start.1), custom_call_target="tpu_custom_call" | custom-call | tf_op jit(solution)/shard_map/solves/pallas_call | solution.py:670
  43.7 1.6 %hand_over.1 = (bf16[3072,256]{1,0:T(8,128)(2,1)}, f32[16,1024]{1,0:T(8,128)}, f32[16,1024]{1,0:T(8,128)}, f32[1024,256]{1,0:T(8,128)}) custom-call(bf16[3,256,1024]{2,1,0:T(8,128)(2,1)S(1)} %get-tuple-element.12.yt, f32[16,1024]{1,0:T(8,128)S(1)} %get-tuple-element.13.rest, f32[16,1024]{1,0:T(8,128)S(1)} %get-tuple-element.14.back, ...), custom_call_target="tpu_custom_call" | custom-call | tf_op jit(solution)/shard_map/hand_over/pallas_call | solution.py:702

commit v5 on v4

--- a/solution.py
+++ b/solution.py
@@ -36,7 +36,7 @@
     yt, rest_out, back_out, vf,
     lv, dv, bv, uv, lt, dt, bt, ut,
     yc, pc, yr, pf, rp, qf, qr, qc, tb, wg, wl, vb,
-    ready, ld_s,
+    ready, joined, ld_s,
     yc_r, pc_r, own_r, s3_r, s4_r, rp_r, qr_r, qc_r, tb_r, ag_r, sib_r,
     y0_s, s1_s, s1b_s, s2_s, s3_s, s4_s, pf_s, ch_s, pc_s, qf_s, qc_s, tb_s, w_s, ag_s, sib_s,
 ):
@@ -61,6 +61,9 @@
     halves = (pl.ds(0, HALF), pl.ds(HALF, HALF))
     mine = pl.ds(pl.multiple_of(group * CHUNK, CHUNK), CHUNK)
 
+    def back_order(step):
+        return jnp.where(step == 3, 3, lax.rem(2 * step, 3))
+
     def remote(src, dst, send, recv, row, col):
         return pltpu.make_async_remote_copy(
             src_ref=src, dst_ref=dst, send_sem=send, recv_sem=recv, device_id=(row, col), device_id_type=MESH
@@ -82,110 +85,139 @@
     loads = [pltpu.make_async_copy(source, target, ld_s.at[k]) for k, (source, target) in enumerate(pairs)]
     for need, load in zip(needs, loads):
         pl.when(need)(load.start)
-    barrier = pltpu.get_barrier_semaphore()
-
-    def greet(row, col):
-        pl.semaphore_signal(barrier, inc=1, device_id=(row, col), device_id_type=MESH)
-
-    def greet_other(row, col):
-        pl.when((row != r) | (col != c))(lambda: greet(row, col))
-
-    @pl.when(chain1)
-    def _():
-        for col in (0, 2, 4, 12):
-            greet(0, col)
-
-    @pl.when(chain20)
-    def _():
-        for col in (6, 8, 13, 14):
-            greet(0, col)
-
-    @pl.when(chain2)
-    def _():
-        greet(1, 0)
-
-    greet(r, c + 1 - 2 * e)
-    loop(7, lambda k: greet(r, lax.rem(c + 2 + 2 * k, 16)))
-    loop(8, lambda k: greet(lax.rem(r + 8, 16), 2 * k + e))
-    pl.when((r == 1) & (c != 0))(lambda: greet(1, 0))
-    pl.when(c != 1)(lambda: greet(r, 1))
-    pl.when(c != 2)(lambda: greet(r, 2))
-    pl.when(r != 13)(lambda: greet(13, c))
-    pl.when(r != 14)(lambda: greet(14, c))
-    pl.when(r != 15)(lambda: greet(15, c))
-
-    def depth(j):
-        return lax.rem(z - j + 8, 8)
-
-    def column(j, far):
-        return yh * 8 + lax.rem(far + j, 8)
-
-    def with_children(j, run):
-        for parent, children in ((0, (2, 7, 1)), (2, (4, 3)), (7, (6,)), (6, (5,))):
-
-            @pl.when(depth(j) == parent)
-            def _():
-                run(children)
-
-    for j in range(STEPS):
-
-        @pl.when(e == SIDE[j])
-        def _():
-            with_children(j, lambda children: [greet(column(j, far), c) for far in children])
-
-    @pl.when(row14 & (c != 13))
-    def _():
-        greet(14, 13)
-
-    @pl.when(row13 & (c != 13))
-    def _():
-        greet(14, 13)
-
-    @pl.when(back1)
-    def _():
-        greet(15, 14)
-
-    pl.when(uses_d)(loads[0].wait)
-
-    @pl.when(row0)
-    def _():
-        loads[1].wait()
-        value = jnp.dot(dv[...], bv[...], preferred_element_type=F32)
-        yr[...] = value.astype(BF16).T
-
-    @pl.when(late)
-    def _():
-        loads[3].wait()
-        ut[...] = uv[...].T
-
-    @pl.when(row15)
-    def _():
-        value = product(ut[...], dv[...])
-        vf[...] = value
-        vb[...] = value.astype(BF16)
-
-    pl.when(uses_l)(loads[2].wait)
-
-    @pl.when(chain1 | chain2)
-    def _():
-        dt[...] = dv[...].T
-
-    @pl.when((c < 3) & (r > c))
-    def _():
-        lt[...] = lv[...].T
-
     def source_of(cols):
         found = c == cols[0]
         for col in cols[1:]:
             found = found | (c == col)
         return row0 & found
 
-    to_one = source_of((0, 2, 4, 12))
-    to_two = source_of((6, 8, 13, 14))
-    count = 16 + jnp.where((c == 1) | (c == 2) | chain1, 15, 0) + jnp.where(late, 15, 0)
+    to_one = source_of((1, 3, 5, 13))
+    to_two = source_of((6, 8, 12, 14))
+    barrier = pltpu.get_barrier_semaphore()
+
+    def greet(row, col):
+        pl.semaphore_signal(barrier, inc=1, device_id=(row, col), device_id_type=MESH)
+
+    def is_early(row, col):
+        return (row == 0) & ((col == 1) | (col == 3) | (col == 5) | (col == 13))
+
+    def meet(run):
+        run(r, c + 1 - 2 * e)
+        loop(7, lambda k: run(r, lax.rem(c + 2 + 2 * k, 16)))
+        loop(8, lambda k: run(lax.rem(r + 8, 16), 2 * k + e))
+
+    def greet_late(row, col):
+        pl.when(jnp.logical_not(is_early(row, col)))(lambda: greet(row, col))
+
+    def join(row, col):
+        @pl.when(is_early(row, col))
+        def _():
+            pl.semaphore_signal(joined, inc=1, device_id=(row, col), device_id_type=MESH)
+
+    @pl.when(chain1)
+    def _():
+        for col in (1, 3, 5, 13):
+            greet(0, col)
+
+    @pl.when(chain20)
+    def _():
+        for col in (6, 8, 12, 14):
+            greet(0, col)
+
+    @pl.when(chain2)
+    def _():
+        greet(1, 0)
+
+    meet(greet_late)
+    pl.when((r == 1) & (c != 0))(lambda: greet(1, 0))
+    pl.when((r > 0) & (c != 1))(lambda: greet(r, 1))
+    pl.when((r > 0) & (c != 2))(lambda: greet(r, 2))
+    pl.when(to_one)(lambda: greet(1, c))
+    pl.when(r != 13)(lambda: greet(13, c))
+    pl.when(r != 14)(lambda: greet(14, c))
+    pl.when(r != 15)(lambda: greet(15, c))
+
+    def depth(j):
+        return lax.rem(z - j + 8, 8)
+
+    def column(j, far):
+        return yh * 8 + lax.rem(far + j, 8)
+
+    def with_children(j, run):
+        for parent, children in ((0, (2, 7, 1)), (2, (4, 3)), (7, (6,)), (6, (5,))):
+
+            @pl.when(depth(j) == parent)
+            def _():
+                run(children)
+
+    for j in range(STEPS):
+
+        @pl.when(e == SIDE[j])
+        def _():
+            with_children(j, lambda children: [greet_late(column(j, far), c) for far in children])
+
+    @pl.when(row14 & (c != 13))
+    def _():
+        greet(14, 13)
+
+    @pl.when(row13 & (c != 13))
+    def _():
+        greet(14, 13)
+
+    @pl.when(back1)
+    def _():
+        greet(15, 14)
+
+    pl.when(uses_d)(loads[0].wait)
+
+    @pl.when(row0)
+    def _():
+        loads[1].wait()
+        value = jnp.dot(dv[...], bv[...], preferred_element_type=F32)
+        yr[...] = value.astype(BF16).T
+
+    @pl.when(late)
+    def _():
+        loads[3].wait()
+        ut[...] = uv[...].T
+
+    @pl.when(row15)
+    def _():
+        value = product(ut[...], dv[...])
+        vf[...] = value
+        vb[...] = value.astype(BF16)
+
+    pl.when(uses_l)(loads[2].wait)
+
+    @pl.when(chain1 | chain2)
+    def _():
+        dt[...] = dv[...].T
+
+    @pl.when((c < 3) & (r > c))
+    def _():
+        lt[...] = lv[...].T
+
+    count = 16 + jnp.where(((c == 1) | (c == 2)) & (r > 0) | chain1, 15, 0) + jnp.where(late, 15, 0)
     count = count + jnp.where(e == 0, jnp.where(z < 2, 1, 2), jnp.where(z == 2, 0, 1))
-    count = count + jnp.where(to_one | to_two | chain1 | (row15 & (c == 14)), 1, 0) + jnp.where(back1, 30, 0)
-    pl.semaphore_wait(barrier, count)
+    count = count + jnp.where(to_two | chain1 | (row15 & (c == 14)), 1, 0) + jnp.where(back1, 30, 0)
+    count = count + jnp.where((r == 1) & ((c == 1) | (c == 3) | (c == 5) | (c == 13)), 1, 0)
+    pl.semaphore_wait(barrier, jnp.where(to_one, 1, count))
+
+    @pl.when(to_one)
+    def _():
+        for col, chunk in ((1, 3), (5, 2), (13, 1), (3, 0)):
+
+            @pl.when(c == col)
+            def _():
+                part = pl.ds(chunk * CHUNK, CHUNK)
+                remote(yr.at[part], yc.at[part], y0_s, yc_r.at[chunk], 1, 0).start()
+
+        pl.semaphore_wait(joined, 14)
+
+    @pl.when(jnp.logical_not(to_one))
+    def _():
+        meet(join)
+        pl.when((r == 1) & (e == 1))(lambda: join(0, c))
 
     for j in range(STEPS):
         near = jnp.where(depth(j) == 5, 6, jnp.where(depth(j) == 6, 7, jnp.where((depth(j) == 4) | (depth(j) == 3), 2, 0)))
@@ -212,14 +244,7 @@
 
     @pl.when(row0)
     def _():
-        for col, chunk in ((0, 3), (4, 2), (12, 1), (2, 0)):
-
-            @pl.when(c == col)
-            def _():
-                part = pl.ds(chunk * CHUNK, CHUNK)
-                remote(yr.at[part], yc.at[part], y0_s, yc_r.at[chunk], 1, 0).start()
-
-        for col, chunk in ((6, 3), (8, 2), (14, 1), (13, 0)):
+        for col, chunk in ((6, 3), (8, 2), (14, 1), (12, 0)):
 
             @pl.when(c == col)
             def _():
@@ -238,7 +263,7 @@
     @pl.when(row15 & (c < 15))
     def _():
         def one(step):
-            chunk = lax.rem(6 - step, 4)
+            chunk = back_order(step)
             part = rows(chunk, CHUNK)
             qf[part] = product(vb[part], lv[...]).astype(BF16)
             for col, target, recv in ((14, qc, qc_r), (13, pc, pc_r)):
@@ -319,6 +344,9 @@
 
         loop(4, one)
 
+    def await_other(j):
+        loop(4, lambda step: got(yt.at[j, rows(3 - step, CHUNK)], s4_r.at[j, 3 - step]))
+
     def apply(j):
         def one(step):
             chunk = 3 - step
@@ -366,7 +394,7 @@
         @pl.when(row14 | row13)
         def _():
             def one(step):
-                chunk = lax.rem(6 - step, 4)
+                chunk = back_order(step)
 
                 @pl.when(chunk == x)
                 def _():
@@ -385,7 +413,7 @@
         @pl.when(row14 | row13)
         def _():
             def one(step):
-                chunk = lax.rem(6 - step, 4)
+                chunk = back_order(step)
                 part = rows(chunk, CHUNK)
                 got(wg.at[chunk, :, 1 - e], sib_r.at[chunk])
                 answer = product(wg[chunk].reshape(CHUNK, NB), dv[...])
@@ -449,7 +477,7 @@
     @pl.when(back1)
     def _():
         def one(step):
-            chunk = lax.rem(6 - step, 4)
+            chunk = back_order(step)
             part = rows(chunk, CHUNK)
             got(qc.at[part], qc_r.at[chunk])
             centred = (ut[part].astype(F32) - qc[part].astype(F32)).astype(BF16)
@@ -480,7 +508,7 @@
     first_two = (jnp.where(z == 1, 1, 0), jnp.where(e == 1, 2, jnp.where(z == 1, 0, 1)))
 
     def below(h):
-        return (h % 8 >= 4) & (h % 8 < 7)
+        return (h % 8 >= 3) & (h % 8 < 7)
 
     @pl.when((e == 0) & jnp.logical_not(row13))
     def _():
@@ -492,11 +520,21 @@
 
     centre()
 
+    @pl.when((e == 0) & row13)
+    def _():
+        spread(0)
+
+    pl.when((e == 1) & row15)(lambda: await_other(0))
+
+    @pl.when((e == 1) & row15 & (c < 15))
+    def _():
+        loop(4, lambda chunk: scatter_qf(chunk, below))
+
     @pl.when(jnp.logical_not(middle))
     def _():
         spread(first_two[1])
 
-    @pl.when(row15 & (c < 15))
+    @pl.when((e == 0) & row15)
     def _():
         loop(4, lambda chunk: scatter_qf(chunk, below))
 
@@ -509,11 +547,11 @@
 
     @pl.when((e == 0) & row13)
     def _():
-        spread(0)
+        spread(1)
 
     solve()
 
-    @pl.when(middle)
+    @pl.when(row14 | (row13 & (e == 1)))
     def _():
         spread(first_two[1])
 
@@ -534,7 +572,7 @@
     @pl.when(e == 1)
     def _():
         collect(2)
-        apply(0)
+        pl.when(jnp.logical_not(row15))(lambda: await_other(0))
         apply(1)
 
     apply(2)
@@ -689,7 +727,7 @@
             pltpu.VMEM((4, 2, 2, PIECE, NB), BF16),
             wide,
             wide,
-            pltpu.SemaphoreType.REGULAR((3,)), dma((4,)),
+            pltpu.SemaphoreType.REGULAR((3,)), pltpu.SemaphoreType.REGULAR, dma((4,)),
             dma((4,)), dma((4,)), dma((3, 2)), dma((3, 4)), dma((3, 4)), dma((3,)), dma((3,)), dma((4,)), dma((2,)),
             dma((4,)), dma((4,)),
             dma(()), dma((4,)), dma((2,)), dma((3,)), dma((3,)), dma((3,)), dma(()), dma((4,)), dma((4,)),

time: 45.5 us -> 43 us (0.945)
  the two profiles are of different devices: /device:TPU:36 before, /device:TPU:195 now
where the time goes in v5:
time: 43 us; the launch traced here: 42.9 us
  Pallas kernels  42.2 us (98%)
  between operations  0.64 us (1%)
    pallas_call x1, Pallas kernels, local(): pl.pallas_call(kernel, name='solves', out_shape=(pltpu.VMEM((STEPS, COLS,...  40.6 us
    pallas_call x1, Pallas kernels, local(): pl.pallas_call(hand_over, name='hand_over', out_shape=(jax.ShapeDtypeStru...  1.62 us

profile of v5, /device:TPU:195, one launch (start us, length us, event | category | flops | bytes accessed | tf_op | source)
XLA Modules:
  0.0 42.9 jit_solution(14079721617792595874)
XLA Ops:
  0.6 40.6 %solves.1 = (bf16[3,256,1024]{2,1,0:T(8,128)(2,1)S(1)}, f32[16,1024]{1,0:T(8,128)S(1)}, f32[16,1024]{1,0:T(8,128)S(1)}, f32[256,1024]{1,0:T(8,128)S(1)}) custom-call(bf16[1024,1024]{1,0:T(8,128)(2,1)} %factor.1, bf16[1024,1024]{1,0:T(8,128)(2,1)} %inverse.1, bf16[1024,256]{1,0:T(8,128)(2,1)} %rhs.1, bf16[1024,256]{1,0:T(8,128)(2,1)} %start.1), custom_call_target="tpu_custom_call" | custom-call | tf_op jit(solution)/shard_map/solves/pallas_call | solution.py:708
  41.2 1.6 %hand_over.1 = (bf16[3072,256]{1,0:T(8,128)(2,1)}, f32[16,1024]{1,0:T(8,128)}, f32[16,1024]{1,0:T(8,128)}, f32[1024,256]{1,0:T(8,128)}) custom-call(bf16[3,256,1024]{2,1,0:T(8,128)(2,1)S(1)} %get-tuple-element.12.yt, f32[16,1024]{1,0:T(8,128)S(1)} %get-tuple-element.13.rest, f32[16,1024]{1,0:T(8,128)S(1)} %get-tuple-element.14.back, ...), custom_call_target="tpu_custom_call" | custom-call | tf_op jit(solution)/shard_map/hand_over/pallas_call | solution.py:740

commit v6 on v5

--- a/solution.py
+++ b/solution.py
@@ -33,9 +33,9 @@
 
 def kernel(
     factor, inverse, rhs, start,
-    yt, rest_out, back_out, vf,
+    so, rest_out, back_out, sl,
     lv, dv, bv, uv, lt, dt, bt, ut,
-    yc, pc, yr, pf, rp, qf, qr, qc, tb, wg, wl, vb,
+    yt, vf, yc, pc, yr, pf, rp, qf, qr, qc, tb, wg, wl, vb,
     ready, joined, ld_s,
     yc_r, pc_r, own_r, s3_r, s4_r, rp_r, qr_r, qc_r, tb_r, ag_r, sib_r,
     y0_s, s1_s, s1b_s, s2_s, s3_s, s4_s, pf_s, ch_s, pc_s, qf_s, qc_s, tb_s, w_s, ag_s, sib_s,
@@ -61,9 +61,6 @@
     halves = (pl.ds(0, HALF), pl.ds(HALF, HALF))
     mine = pl.ds(pl.multiple_of(group * CHUNK, CHUNK), CHUNK)
 
-    def back_order(step):
-        return jnp.where(step == 3, 3, lax.rem(2 * step, 3))
-
     def remote(src, dst, send, recv, row, col):
         return pltpu.make_async_remote_copy(
             src_ref=src, dst_ref=dst, send_sem=send, recv_sem=recv, device_id=(row, col), device_id_type=MESH
@@ -83,8 +80,8 @@
     needs = (uses_d, r >= 0, uses_l, late)
     pairs = ((inverse, dv), (rhs, bv), (factor, lv), (start, uv))
     loads = [pltpu.make_async_copy(source, target, ld_s.at[k]) for k, (source, target) in enumerate(pairs)]
-    for need, load in zip(needs, loads):
-        pl.when(need)(load.start)
+    for k in (0, 3, 1, 2):
+        pl.when(needs[k])(loads[k].start)
     def source_of(cols):
         found = c == cols[0]
         for col in cols[1:]:
@@ -181,12 +178,13 @@
         loads[3].wait()
         ut[...] = uv[...].T
 
-    @pl.when(row15)
-    def _():
-        value = product(ut[...], dv[...])
-        vf[...] = value
-        vb[...] = value.astype(BF16)
-
+    def solve_15(step):
+        part = rows(step, 2 * CHUNK)
+        value = product(ut[part], dv[...])
+        vf[part] = value
+        vb[part] = value.astype(BF16)
+
+    pl.when(row15)(lambda: solve_15(0))
     pl.when(uses_l)(loads[2].wait)
 
     @pl.when(chain1 | chain2)
@@ -260,17 +258,21 @@
                 remote(yr.at[part, side], yt.at[0, part, side], s1_s.at[0], own_r.at[0, k], *to).start()
             yt[0, mine] = yr[mine]
 
-    @pl.when(row15 & (c < 15))
+    @pl.when(row15)
     def _():
         def one(step):
-            chunk = back_order(step)
-            part = rows(chunk, CHUNK)
-            qf[part] = product(vb[part], lv[...]).astype(BF16)
+            part = rows(step, CHUNK)
+            pl.when(step == 2)(lambda: solve_15(1))
+
+            @pl.when(c < 15)
+            def _():
+                qf[part] = product(vb[part], lv[...]).astype(BF16)
+
             for col, target, recv in ((14, qc, qc_r), (13, pc, pc_r)):
 
                 @pl.when(c == col)
                 def _():
-                    remote(qf.at[part], target.at[part], qc_s.at[chunk], recv.at[chunk], 14, 13).start()
+                    remote(qf.at[part], target.at[part], qc_s.at[step], recv.at[step], 14, 13).start()
 
         loop(4, one)
 
@@ -349,26 +351,31 @@
 
     def apply(j):
         def one(step):
-            chunk = 3 - step
-            part = rows(chunk, CHUNK)
+            part = rows(1 - step, 2 * CHUNK)
+            pair = (3 - 2 * step, 2 - 2 * step)
 
             @pl.when(e != SIDE[j])
             def _():
-                got(yt.at[j, part], s4_r.at[j, chunk])
+                for chunk in pair:
+                    got(yt.at[j, rows(chunk, CHUNK)], s4_r.at[j, chunk])
 
             @pl.when((c == j) & (r >= 3))
             def _():
                 partial = product(yt[j, part], lt[...]).astype(BF16)
                 if j == 1:
-                    got(pc.at[part], pc_r.at[chunk])
+                    for chunk in pair:
+                        got(pc.at[rows(chunk, CHUNK)], pc_r.at[chunk])
                     partial = (pc[part].astype(F32) + partial.astype(F32)).astype(BF16)
                 pf[part] = partial
-                if j == 0:
-                    remote(pf.at[part], pc.at[part], pc_s.at[chunk], pc_r.at[chunk], r, 1).start()
-                else:
-                    scatter_pf(chunk)
-
-        loop(4, one)
+                for chunk in pair:
+                    if j == 0:
+                        half = rows(chunk, CHUNK)
+                        remote(pf.at[half], pc.at[half], pc_s.at[chunk], pc_r.at[chunk], r, 1).start()
+                    else:
+                        scatter_pf(chunk)
+
+        loop(2, one)
+        so[pl.ds(j * NB, NB)] = yt[j].T
 
     def centre():
         block = wg.at[x, yl, e]
@@ -390,11 +397,10 @@
 
             loop(7, one)
 
-    def gather():
-        @pl.when(row14 | row13)
-        def _():
-            def one(step):
-                chunk = back_order(step)
+    def gather_and_solve(between):
+        def one(step):
+            for k in range(2):
+                chunk = 2 * step + k
 
                 @pl.when(chunk == x)
                 def _():
@@ -407,28 +413,25 @@
                 block = wg.at[chunk, :, e]
                 remote(block, block, sib_s.at[chunk], sib_r.at[chunk], r, c + 1 - 2 * e).start()
 
-            loop(4, one)
-
-    def solve():
-        @pl.when(row14 | row13)
-        def _():
-            def one(step):
-                chunk = back_order(step)
-                part = rows(chunk, CHUNK)
-                got(wg.at[chunk, :, 1 - e], sib_r.at[chunk])
-                answer = product(wg[chunk].reshape(CHUNK, NB), dv[...])
-                vf[part] = answer
-
-                @pl.when((c < r) & jnp.logical_not(back1))
-                def _():
-                    qf[part] = product(answer.astype(BF16), lv[...]).astype(BF16)
-                    scatter_qf(chunk)
-
-            loop(4, one)
-
-            @pl.when(back1)
-            def _():
-                loop(4, scatter_qf)
+            part = rows(step, 2 * CHUNK)
+            for k in range(2):
+                got(wg.at[2 * step + k, :, 1 - e], sib_r.at[2 * step + k])
+            answer = product(wg[pl.ds(2 * step, 2)].reshape(2 * CHUNK, NB), dv[...])
+            vf[part] = answer
+
+            @pl.when((c < r) & jnp.logical_not(back1))
+            def _():
+                qf[part] = product(answer.astype(BF16), lv[...]).astype(BF16)
+
+            @pl.when(c < r)
+            def _():
+                scatter_qf(2 * step)
+                scatter_qf(2 * step + 1)
+
+            pl.when((step == 0) & (e == 0))(between)
+
+        loop(2, one)
+        pl.when(e == 1)(between)
 
     @pl.when(chain1)
     def _():
@@ -477,7 +480,7 @@
     @pl.when(back1)
     def _():
         def one(step):
-            chunk = back_order(step)
+            chunk = step
             part = rows(chunk, CHUNK)
             got(qc.at[part], qc_r.at[chunk])
             centred = (ut[part].astype(F32) - qc[part].astype(F32)).astype(BF16)
@@ -543,17 +546,9 @@
         collect(0)
         apply(0)
 
-    gather()
-
-    @pl.when((e == 0) & row13)
-    def _():
-        spread(1)
-
-    solve()
-
-    @pl.when(row14 | (row13 & (e == 1)))
-    def _():
-        spread(first_two[1])
+    @pl.when(middle)
+    def _():
+        gather_and_solve(lambda: spread(first_two[1]))
 
     @pl.when((e == 0) & middle)
     def _():
@@ -573,9 +568,18 @@
     def _():
         collect(2)
         pl.when(jnp.logical_not(row15))(lambda: await_other(0))
+        so[pl.ds(0, NB)] = yt[0].T
         apply(1)
 
     apply(2)
+
+    @pl.when(late)
+    def _():
+        sl[...] = vf[...].T
+
+    @pl.when(jnp.logical_not(late))
+    def _():
+        sl[...] = jnp.zeros_like(sl)
 
     for j in range(STEPS):
 
@@ -672,30 +676,13 @@
                 back_out[...] += qr[j].astype(F32)
 
 
-def hand_over(yt, rest, back, vf, solved_out, rest_out, back_out, solution_out, so, sl, sems):
-    late = lax.axis_index("row") >= 13
-    answer = pltpu.make_async_copy(sl, solution_out, sems.at[5])
-    stores = [pltpu.make_async_copy(rest, rest_out, sems.at[3]), pltpu.make_async_copy(back, back_out, sems.at[4])]
-    for store in stores:
-        store.start()
-
-    @pl.when(jnp.logical_not(late))
-    def _():
-        sl[...] = jnp.zeros_like(sl)
-
-    @pl.when(late)
-    def _():
-        sl[...] = vf[...].T
-
-    answer.start()
-    for j in range(STEPS):
-        whole = pl.ds(j * NB, NB)
-        so[whole] = yt[j].T
-        stores.append(pltpu.make_async_copy(so.at[whole], solved_out.at[whole], sems.at[j]))
-        stores[-1].start()
-    for store in stores:
-        store.wait()
-    answer.wait()
+def hand_over(*refs):
+    sems = refs[-1]
+    copies = [pltpu.make_async_copy(refs[k], refs[k + 4], sems.at[k]) for k in range(4)]
+    for copy in copies:
+        copy.start()
+    for copy in copies:
+        copy.wait()
 
 
 def local(factor, diag_inv, rhs, forward_values):
@@ -709,15 +696,17 @@
         kernel,
         name="solves",
         out_shape=(
-            pltpu.VMEM((STEPS, COLS, NB), BF16),
+            pltpu.VMEM((STEPS * NB, COLS), BF16),
             pltpu.VMEM((PIECE, NB), F32),
             pltpu.VMEM((PIECE, NB), F32),
-            pltpu.VMEM((COLS, NB), F32),
+            pltpu.VMEM((NB, COLS), F32),
         ),
         in_specs=[anywhere] * 4,
         out_specs=(vmem,) * 4,
         scratch_shapes=[
             square, square, tall, tall, square, square, wide, wide,
+            pltpu.VMEM((STEPS, COLS, NB), BF16),
+            pltpu.VMEM((COLS, NB), F32),
             wide, wide, wide, wide,
             pltpu.VMEM((STEPS, PIECE, NB), BF16),
             wide,
@@ -748,7 +737,7 @@
         ),
         in_specs=[vmem] * 4,
         out_specs=(anywhere,) * 4,
-        scratch_shapes=[pltpu.VMEM((STEPS * NB, COLS), BF16), pltpu.VMEM((NB, COLS), F32), dma((6,))],
+        scratch_shapes=[dma((4,))],
         compiler_params=pltpu.CompilerParams(vmem_limit_bytes=32 * 1024 * 1024),
     )(*results)
     return solved, rest.T, back.T, answer

time: 43 us -> 41.6 us (0.967)
  the two profiles are of different devices: /device:TPU:195 before, /device:TPU:57 now
where the time goes in v6:
time: 41.6 us; the launch traced here: 41.5 us
  Pallas kernels  40.8 us (98%)
  between operations  0.64 us (2%)
    pallas_call x1, Pallas kernels, local(): pl.pallas_call(kernel, name='solves', out_shape=(pltpu.VMEM((STEPS * NB,...  39.3 us
    pallas_call x1, Pallas kernels, local(): pl.pallas_call(hand_over, name='hand_over', out_shape=(jax.ShapeDtypeStru...  1.57 us

profile of v6, /device:TPU:57, one launch (start us, length us, event | category | flops | bytes accessed | tf_op | source)
XLA Modules:
  0.0 41.5 jit_solution(1664757185353739079)
XLA Ops:
  0.6 39.3 %solves.1 = (bf16[3072,256]{1,0:T(8,128)(2,1)S(1)}, f32[16,1024]{1,0:T(8,128)S(1)}, f32[16,1024]{1,0:T(8,128)S(1)}, f32[1024,256]{1,0:T(8,128)S(1)}) custom-call(bf16[1024,1024]{1,0:T(8,128)(2,1)} %factor.1, bf16[1024,1024]{1,0:T(8,128)(2,1)} %inverse.1, bf16[1024,256]{1,0:T(8,128)(2,1)} %rhs.1, bf16[1024,256]{1,0:T(8,128)(2,1)} %start.1), custom_call_target="tpu_custom_call" | custom-call | tf_op jit(solution)/shard_map/solves/pallas_call | solution.py:695
  39.9 1.6 %hand_over.1 = (bf16[3072,256]{1,0:T(8,128)(2,1)}, f32[16,1024]{1,0:T(8,128)}, f32[16,1024]{1,0:T(8,128)}, f32[1024,256]{1,0:T(8,128)}) custom-call(bf16[3072,256]{1,0:T(8,128)(2,1)S(1)} %get-tuple-element.12.refs_0_, f32[16,1024]{1,0:T(8,128)S(1)} %get-tuple-element.13.refs_1_, f32[16,1024]{1,0:T(8,128)S(1)} %get-tuple-element.14.refs_2_, ...), custom_call_target="tpu_custom_call" | custom-call | tf_op jit(solution)/shard_map/hand_over/pallas_call | solution.py:729

commit v7 on v6

--- a/solution.py
+++ b/solution.py
@@ -13,6 +13,7 @@
 PIECE = 16
 CHUNK = 64
 HALF = 512
+TILE = 256
 SIDE = (0, 0, 1)
 MESH = pl.DeviceIdType.MESH
 F32 = jnp.float32
@@ -21,6 +22,20 @@
 
 def product(left, right):
     return lax.dot_general(left, right, (((1,), (0,)), ((), ())), preferred_element_type=F32)
+
+
+def times_lower(left, block):
+    parts = []
+    for k in range(0, NB, TILE):
+        parts.append(product(left[:, k:], block[pl.ds(k, NB - k), pl.ds(k, TILE)]))
+    return jnp.concatenate(parts, axis=1)
+
+
+def times_upper(left, block):
+    parts = []
+    for k in range(0, NB, TILE):
+        parts.append(product(left[:, : k + TILE], block[pl.ds(0, k + TILE), pl.ds(k, TILE)]))
+    return jnp.concatenate(parts, axis=1)
 
 
 def loop(count, body):
@@ -61,6 +76,9 @@
     halves = (pl.ds(0, HALF), pl.ds(HALF, HALF))
     mine = pl.ds(pl.multiple_of(group * CHUNK, CHUNK), CHUNK)
 
+    def swap(index):
+        return jnp.where(index == 1, 2, jnp.where(index == 2, 1, index))
+
     def remote(src, dst, send, recv, row, col):
         return pltpu.make_async_remote_copy(
             src_ref=src, dst_ref=dst, send_sem=send, recv_sem=recv, device_id=(row, col), device_id_type=MESH
@@ -170,8 +188,10 @@
     @pl.when(row0)
     def _():
         loads[1].wait()
-        value = jnp.dot(dv[...], bv[...], preferred_element_type=F32)
-        yr[...] = value.astype(BF16).T
+        for k in range(0, NB, TILE):
+            span = pl.ds(k, TILE)
+            value = product(dv[span, pl.ds(0, k + TILE)], bv[pl.ds(0, k + TILE)])
+            yr[:, span] = value.astype(BF16).T
 
     @pl.when(late)
     def _():
@@ -180,7 +200,7 @@
 
     def solve_15(step):
         part = rows(step, 2 * CHUNK)
-        value = product(ut[part], dv[...])
+        value = times_lower(ut[part], dv)
         vf[part] = value
         vb[part] = value.astype(BF16)
 
@@ -261,8 +281,9 @@
     @pl.when(row15)
     def _():
         def one(step):
-            part = rows(step, CHUNK)
-            pl.when(step == 2)(lambda: solve_15(1))
+            chunk = swap(step)
+            part = rows(chunk, CHUNK)
+            pl.when(step == 1)(lambda: solve_15(1))
 
             @pl.when(c < 15)
             def _():
@@ -272,7 +293,7 @@
 
                 @pl.when(c == col)
                 def _():
-                    remote(qf.at[part], target.at[part], qc_s.at[step], recv.at[step], 14, 13).start()
+                    remote(qf.at[part], target.at[part], qc_s.at[chunk], recv.at[chunk], 14, 13).start()
 
         loop(4, one)
 
@@ -297,39 +318,69 @@
     heads = ((x < 2) & (y < 2), ((x == 0) | (x == 3)) & ((y == 0) | (y == 3)))
 
     def spread(j):
-        local = (row0 & (j == 0)) | (chain1 & (j == 1)) | (chain2 & (j == 2))
+        root = (chain1 & (j == 1)) | (chain2 & (j == 2))
+        local = root | (row0 & (j == 0))
         starts = (z == j) & (j > 0)
         turned = starts & heads[1] & jnp.logical_not(heads[0])
 
+        def part_of(side):
+            return yt.at[j, mine, pl.ds(pl.multiple_of(side * HALF, HALF), HALF)]
+
+        def to_chip(side, send, recv, tx, ty):
+            part = part_of(side)
+            remote(part, part, send, recv, 8 * (ty // 2) + z, 4 * tx + 2 * (ty % 2) + e).start()
+
+        def around(side):
+            x2, y2 = lax.rem(x + 2, 4), lax.rem(y + 2, 4)
+            to_chip(side, s1b_s.at[side], own_r.at[j, side], x2, y2)
+            to_chip(side, s1b_s.at[side], own_r.at[j, side], x2, y)
+            to_chip(side, s1b_s.at[side], own_r.at[j, side], x, y2)
+
+        def along(side, opening):
+            def run(children):
+                if opening:
+                    pl.semaphore_wait(ready.at[j], len(children))
+                part = part_of(side)
+                for far in children:
+                    remote(part, part, s2_s.at[j], own_r.at[j, side], column(j, far), c).start()
+
+            with_children(j, run)
+
+        def across(side):
+            x1, y1 = lax.rem(x + 1 + 2 * side, 4), lax.rem(y + 1 + 2 * side, 4)
+            to_chip(side, s3_s.at[j], s3_r.at[j, group], x1, y1)
+            to_chip(side, s3_s.at[j], s3_r.at[j, group], x1, y)
+            to_chip(side, s3_s.at[j], s3_r.at[j, group], x, y1)
+
         for step in range(2):
             side = jnp.where(turned, 1 - step, step)
-            part = yt.at[j, mine, pl.ds(pl.multiple_of(side * HALF, HALF), HALF)]
-
-            def to_chip(send, recv, tx, ty):
-                remote(part, part, send, recv, 8 * (ty // 2) + z, 4 * tx + 2 * (ty % 2) + e).start()
 
             @pl.when(jnp.logical_not(local))
             def _():
-                got(part, own_r.at[j, side])
+                got(part_of(side), own_r.at[j, side])
 
             @pl.when(starts & jnp.where(side == 0, heads[0], heads[1]))
             def _():
-                x2, y2 = lax.rem(x + 2, 4), lax.rem(y + 2, 4)
-                to_chip(s1b_s.at[side], own_r.at[j, side], x2, y2)
-                to_chip(s1b_s.at[side], own_r.at[j, side], x2, y)
-                to_chip(s1b_s.at[side], own_r.at[j, side], x, y2)
-
-            def run(children):
-                if step == 0:
-                    pl.semaphore_wait(ready.at[j], len(children))
-                for far in children:
-                    remote(part, part, s2_s.at[j], own_r.at[j, side], column(j, far), c).start()
-
-            with_children(j, run)
-            x1, y1 = lax.rem(x + 1 + 2 * side, 4), lax.rem(y + 1 + 2 * side, 4)
-            to_chip(s3_s.at[j], s3_r.at[j, group], x1, y1)
-            to_chip(s3_s.at[j], s3_r.at[j, group], x1, y)
-            to_chip(s3_s.at[j], s3_r.at[j, group], x, y1)
+                around(side)
+
+            @pl.when(jnp.logical_not(root))
+            def _():
+                along(side, step == 0)
+                across(side)
+
+        @pl.when(root)
+        def _():
+            @pl.when(chain1)
+            def _():
+                for k in range(4):
+                    sent(yr.at[pl.ds(0, CHUNK)], ch_s.at[k])
+
+            for side in range(2):
+                along(side, side == 0)
+            for side in range(2):
+                sent(yt.at[0, pl.ds(0, 192), halves[side]], s1b_s.at[side])
+            for side in range(2):
+                across(side)
 
         block = yt.at[j, mine]
         remote(block, block, s4_s.at[j], s4_r.at[j, group], r, c + 1 - 2 * e).start()
@@ -397,10 +448,10 @@
 
             loop(7, one)
 
-    def gather_and_solve(between):
+    def gather_and_solve():
         def one(step):
-            for k in range(2):
-                chunk = 2 * step + k
+            pair = (step, step + 2)
+            for chunk in pair:
 
                 @pl.when(chunk == x)
                 def _():
@@ -413,25 +464,33 @@
                 block = wg.at[chunk, :, e]
                 remote(block, block, sib_s.at[chunk], sib_r.at[chunk], r, c + 1 - 2 * e).start()
 
-            part = rows(step, 2 * CHUNK)
-            for k in range(2):
-                got(wg.at[2 * step + k, :, 1 - e], sib_r.at[2 * step + k])
-            answer = product(wg[pl.ds(2 * step, 2)].reshape(2 * CHUNK, NB), dv[...])
-            vf[part] = answer
+            for chunk in pair:
+                got(wg.at[chunk, :, 1 - e], sib_r.at[chunk])
+            operand = jnp.concatenate([wg[chunk].reshape(CHUNK, NB) for chunk in pair], axis=0)
+            answer = times_lower(operand, dv)
+            for k, chunk in enumerate(pair):
+                vf[rows(chunk, CHUNK)] = answer[k * CHUNK:(k + 1) * CHUNK]
 
             @pl.when((c < r) & jnp.logical_not(back1))
             def _():
-                qf[part] = product(answer.astype(BF16), lv[...]).astype(BF16)
+                partial = product(answer.astype(BF16), lv[...]).astype(BF16)
+                for k, chunk in enumerate(pair):
+                    qf[rows(chunk, CHUNK)] = partial[k * CHUNK:(k + 1) * CHUNK]
 
             @pl.when(c < r)
             def _():
-                scatter_qf(2 * step)
-                scatter_qf(2 * step + 1)
-
-            pl.when((step == 0) & (e == 0))(between)
+                for chunk in pair:
+                    scatter_qf(chunk)
+
+            @pl.when((step == 0) & (e == 0))
+            def _():
+                spread(1)
 
         loop(2, one)
-        pl.when(e == 1)(between)
+
+        @pl.when(e == 1)
+        def _():
+            spread(2)
 
     @pl.when(chain1)
     def _():
@@ -442,7 +501,7 @@
             partial = product(yc[part], lt[...]).astype(BF16)
             pf[part] = partial
             residue = (bt[part].astype(F32) - partial.astype(F32)).astype(BF16)
-            yr[part] = product(residue, dt[...]).astype(BF16)
+            yr[part] = times_upper(residue, dt).astype(BF16)
             remote(yr.at[part], yc.at[part], ch_s.at[chunk], yc_r.at[chunk], 2, 1).start()
             for k in range(4):
                 pl.when(chunk == k)(lambda: scatter_s1(1, k))
@@ -471,7 +530,7 @@
             total = pc[part].astype(F32) + partial.astype(F32)
             pf[part] = total.astype(BF16)
             residue = (bt[part].astype(F32) - total).astype(BF16)
-            yr[part] = product(residue, dt[...]).astype(BF16)
+            yr[part] = times_upper(residue, dt).astype(BF16)
             for k in range(4):
                 pl.when(chunk == k)(lambda: scatter_s1(2, k))
 
@@ -480,31 +539,33 @@
     @pl.when(back1)
     def _():
         def one(step):
-            chunk = step
+            chunk = swap(step)
             part = rows(chunk, CHUNK)
             got(qc.at[part], qc_r.at[chunk])
             centred = (ut[part].astype(F32) - qc[part].astype(F32)).astype(BF16)
             wl[part] = centred
-            answer = product(centred, dv[...]).astype(BF16)
+            for k in range(4):
+                piece = rows(4 * chunk + k, PIECE)
+                to = 4 * chunk + k
+                target = wg.at[chunk, k // 2, k % 2]
+
+                @pl.when(to != c)
+                def _():
+                    remote(wl.at[piece], target, w_s, tb_r.at[0], 14, to).start()
+
+                @pl.when(to == c)
+                def _():
+                    target[...] = wl[piece]
+
+            answer = times_lower(centred, dv).astype(BF16)
             partial = product(answer, lv[...]).astype(BF16)
             qf[part] = partial
             got(pc.at[part], pc_r.at[chunk])
             yc[part] = (pc[part].astype(F32) + partial.astype(F32)).astype(BF16)
             for k in range(4):
-                g = 4 * chunk + k
-                remote(yc.at[rows(g, PIECE)], tb, tb_s, tb_r.at[0], 13, g).start()
-            for k in range(4):
                 piece = rows(4 * chunk + k, PIECE)
-                target = wg.at[chunk, k // 2, k % 2]
-
-                @pl.when(4 * chunk + k != c)
-                def _():
-                    remote(wl.at[piece], target, w_s, tb_r.at[0], 14, 4 * chunk + k).start()
-
-                @pl.when(4 * chunk + k == c)
-                def _():
-                    target[...] = wl[piece]
-
+                to = 4 * chunk + k
+                remote(yc.at[piece], tb, tb_s, tb_r.at[0], 13, to).start()
         loop(4, one)
 
     middle = row13 | row14
@@ -548,7 +609,7 @@
 
     @pl.when(middle)
     def _():
-        gather_and_solve(lambda: spread(first_two[1]))
+        gather_and_solve()
 
     @pl.when((e == 0) & middle)
     def _():
@@ -591,7 +652,7 @@
 
     for k in range(2):
 
-        @pl.when(((z == 1) & (e == 0) | (z == 2) & (e == 1)) & heads[k])
+        @pl.when(((z == 1) & (e == 0) | (z == 2) & (e == 1)) & heads[k] & jnp.logical_not(chain1 | chain2))
         def _():
             sent(yt.at[0, pl.ds(0, 192), halves[k]], s1b_s.at[k])
 
@@ -609,11 +670,6 @@
     def _():
         for k in range(1, 4):
             sent(yr.at[pl.ds(0, CHUNK)], s1_s.at[k])
-
-    @pl.when(chain1)
-    def _():
-        for k in range(4):
-            sent(yr.at[pl.ds(0, CHUNK)], ch_s.at[k])
 
     @pl.when((c == 0) & (r >= 2))
     def _():

time: 41.6 us -> 40.6 us (0.976)
  Pallas kernels: 40.8 us -> 39.9 us
    pallas_call x1, Pallas kernels: 39.3 us -> 38.3 us  [local(): pl.pallas_call(kernel, name='solves', out_shape=(pltpu.VMEM((STEPS * NB,...]
where the time goes in v7:
time: 40.6 us; the launch traced here: 40.5 us
  Pallas kernels  39.9 us (98%)
  between operations  0.64 us (2%)
    pallas_call x1, Pallas kernels, local(): pl.pallas_call(kernel, name='solves', out_shape=(pltpu.VMEM((STEPS * NB,...  38.3 us
    pallas_call x1, Pallas kernels, local(): pl.pallas_call(hand_over, name='hand_over', out_shape=(jax.ShapeDtypeStru...  1.57 us

profile of v7, /device:TPU:57, one launch (start us, length us, event | category | flops | bytes accessed | tf_op | source)
XLA Modules:
  0.0 40.5 jit_solution(7472547941488963684)
XLA Ops:
  0.6 38.3 %solves.1 = (bf16[3072,256]{1,0:T(8,128)(2,1)S(1)}, f32[16,1024]{1,0:T(8,128)S(1)}, f32[16,1024]{1,0:T(8,128)S(1)}, f32[1024,256]{1,0:T(8,128)S(1)}) custom-call(bf16[1024,1024]{1,0:T(8,128)(2,1)} %factor.1, bf16[1024,1024]{1,0:T(8,128)(2,1)} %inverse.1, bf16[1024,256]{1,0:T(8,128)(2,1)} %rhs.1, bf16[1024,256]{1,0:T(8,128)(2,1)} %start.1), custom_call_target="tpu_custom_call" | custom-call | tf_op jit(solution)/shard_map/solves/pallas_call | solution.py:751
  39.0 1.6 %hand_over.1 = (bf16[3072,256]{1,0:T(8,128)(2,1)}, f32[16,1024]{1,0:T(8,128)}, f32[16,1024]{1,0:T(8,128)}, f32[1024,256]{1,0:T(8,128)}) custom-call(bf16[3072,256]{1,0:T(8,128)(2,1)S(1)} %get-tuple-element.12.refs_0_, f32[16,1024]{1,0:T(8,128)S(1)} %get-tuple-element.13.refs_1_, f32[16,1024]{1,0:T(8,128)S(1)} %get-tuple-element.14.refs_2_, ...), custom_call_target="tpu_custom_call" | custom-call | tf_op jit(solution)/shard_map/hand_over/pallas_call | solution.py:785

commit v8 on v7

--- a/solution.py
+++ b/solution.py
@@ -52,9 +52,10 @@
     lv, dv, bv, uv, lt, dt, bt, ut,
     yt, vf, yc, pc, yr, pf, rp, qf, qr, qc, tb, wg, wl, vb,
     ready, joined, ld_s,
-    yc_r, pc_r, own_r, s3_r, s4_r, rp_r, qr_r, qc_r, tb_r, ag_r, sib_r,
-    y0_s, s1_s, s1b_s, s2_s, s3_s, s4_s, pf_s, ch_s, pc_s, qf_s, qc_s, tb_s, w_s, ag_s, sib_s,
+    yc_r, pc_r, own_r, s3_r, s4_r, rp_r, qr_r, tb_r, ag_r, sib_r,
+    y0_s, s1_s, s1b_s, s2_s, s3_s, s4_s, pf_s, ch_s, qf_s, w_s, ag_s,
 ):
+    qc_r, pc_s, qc_s, sib_s, tb_s = yc_r, ch_s, ch_s, s1_s, y0_s
     r = lax.axis_index("row")
     c = lax.axis_index("col")
     x = c // 4
@@ -242,7 +243,7 @@
 
         @pl.when((e == SIDE[j]) & (depth(j) != 0))
         def _():
-            pl.semaphore_signal(ready.at[j], inc=1, device_id=(column(j, near), c), device_id_type=MESH)
+            pl.semaphore_signal(ready.at[j % 2], inc=1, device_id=(column(j, near), c), device_id_type=MESH)
 
     def scatter_pf(chunk):
         for k in range(4):
@@ -313,7 +314,7 @@
             far = pl.ds(side * HALF, HALF)
             row = j + (8 * b if side else 0)
             col = (12 * a if side else 4 * a) + 2 * b + SIDE[j]
-            remote(yr.at[part, far], yt.at[j, part, far], s1_s.at[chunk], own_r.at[j, side], row, col).start()
+            remote(yr.at[part, far], yt.at[j, part, far], s1_s.at[chunk], own_r.at[j % 2, side], row, col).start()
 
     heads = ((x < 2) & (y < 2), ((x == 0) | (x == 3)) & ((y == 0) | (y == 3)))
 
@@ -332,32 +333,32 @@
 
         def around(side):
             x2, y2 = lax.rem(x + 2, 4), lax.rem(y + 2, 4)
-            to_chip(side, s1b_s.at[side], own_r.at[j, side], x2, y2)
-            to_chip(side, s1b_s.at[side], own_r.at[j, side], x2, y)
-            to_chip(side, s1b_s.at[side], own_r.at[j, side], x, y2)
+            to_chip(side, s1b_s.at[side], own_r.at[j % 2, side], x2, y2)
+            to_chip(side, s1b_s.at[side], own_r.at[j % 2, side], x2, y)
+            to_chip(side, s1b_s.at[side], own_r.at[j % 2, side], x, y2)
 
         def along(side, opening):
             def run(children):
                 if opening:
-                    pl.semaphore_wait(ready.at[j], len(children))
+                    pl.semaphore_wait(ready.at[j % 2], len(children))
                 part = part_of(side)
                 for far in children:
-                    remote(part, part, s2_s.at[j], own_r.at[j, side], column(j, far), c).start()
+                    remote(part, part, s2_s.at[j % 2], own_r.at[j % 2, side], column(j, far), c).start()
 
             with_children(j, run)
 
         def across(side):
             x1, y1 = lax.rem(x + 1 + 2 * side, 4), lax.rem(y + 1 + 2 * side, 4)
-            to_chip(side, s3_s.at[j], s3_r.at[j, group], x1, y1)
-            to_chip(side, s3_s.at[j], s3_r.at[j, group], x1, y)
-            to_chip(side, s3_s.at[j], s3_r.at[j, group], x, y1)
+            to_chip(side, s3_s.at[j % 2], s3_r.at[j % 2, group], x1, y1)
+            to_chip(side, s3_s.at[j % 2], s3_r.at[j % 2, group], x1, y)
+            to_chip(side, s3_s.at[j % 2], s3_r.at[j % 2, group], x, y1)
 
         for step in range(2):
             side = jnp.where(turned, 1 - step, step)
 
             @pl.when(jnp.logical_not(local))
             def _():
-                got(part_of(side), own_r.at[j, side])
+                got(part_of(side), own_r.at[j % 2, side])
 
             @pl.when(starts & jnp.where(side == 0, heads[0], heads[1]))
             def _():
@@ -383,7 +384,7 @@
                 across(side)
 
         block = yt.at[j, mine]
-        remote(block, block, s4_s.at[j], s4_r.at[j, group], r, c + 1 - 2 * e).start()
+        remote(block, block, s4_s.at[j % 2], s4_r.at[j % 2, group], r, c + 1 - 2 * e).start()
 
     def collect(j):
         def one(step):
@@ -392,13 +393,13 @@
 
             @pl.when(chunk != group)
             def _():
-                got(block, s3_r.at[j, chunk])
-                remote(block, block, s4_s.at[j], s4_r.at[j, chunk], r, c + 1 - 2 * e).start()
+                got(block, s3_r.at[j % 2, chunk])
+                remote(block, block, s4_s.at[j % 2], s4_r.at[j % 2, chunk], r, c + 1 - 2 * e).start()
 
         loop(4, one)
 
     def await_other(j):
-        loop(4, lambda step: got(yt.at[j, rows(3 - step, CHUNK)], s4_r.at[j, 3 - step]))
+        loop(4, lambda step: got(yt.at[j, rows(3 - step, CHUNK)], s4_r.at[j % 2, 3 - step]))
 
     def apply(j):
         def one(step):
@@ -408,7 +409,7 @@
             @pl.when(e != SIDE[j])
             def _():
                 for chunk in pair:
-                    got(yt.at[j, rows(chunk, CHUNK)], s4_r.at[j, chunk])
+                    got(yt.at[j, rows(chunk, CHUNK)], s4_r.at[j % 2, chunk])
 
             @pl.when((c == j) & (r >= 3))
             def _():
@@ -442,11 +443,9 @@
 
         @pl.when(row14 | row13)
         def _():
-            def one(k):
-                to = lax.rem(2 * x + yl + 1 + k, 8)
+            for ahead in (4, 5, 3, 2, 6, 7, 1):
+                to = lax.rem(2 * x + yl + ahead, 8)
                 remote(block, block, ag_s, ag_r.at[x], r, 2 * to + e).start()
-
-            loop(7, one)
 
     def gather_and_solve():
         def one(step):
@@ -646,9 +645,9 @@
 
         @pl.when(e == SIDE[j])
         def _():
-            sent(yt.at[j, pl.ds(0, 192)], s3_s.at[j])
-            sent(yt.at[j], s4_s.at[j])
-            with_children(j, lambda children: sent(yt.at[j, pl.ds(0, len(children) * CHUNK)], s2_s.at[j]))
+            sent(yt.at[j, pl.ds(0, 192)], s3_s.at[j % 2])
+            sent(yt.at[j], s4_s.at[j % 2])
+            with_children(j, lambda children: sent(yt.at[j, pl.ds(0, len(children) * CHUNK)], s2_s.at[j % 2]))
 
     for k in range(2):
 
@@ -772,11 +771,9 @@
             pltpu.VMEM((4, 2, 2, PIECE, NB), BF16),
             wide,
             wide,
-            pltpu.SemaphoreType.REGULAR((3,)), pltpu.SemaphoreType.REGULAR, dma((4,)),
-            dma((4,)), dma((4,)), dma((3, 2)), dma((3, 4)), dma((3, 4)), dma((3,)), dma((3,)), dma((4,)), dma((2,)),
-            dma((4,)), dma((4,)),
-            dma(()), dma((4,)), dma((2,)), dma((3,)), dma((3,)), dma((3,)), dma(()), dma((4,)), dma((4,)),
-            dma(()), dma((4,)), dma(()), dma(()), dma(()), dma((4,)),
+            pltpu.SemaphoreType.REGULAR((2,)), pltpu.SemaphoreType.REGULAR, dma((4,)),
+            dma((4,)), dma((4,)), dma((2, 2)), dma((2, 4)), dma((2, 4)), dma((3,)), dma((3,)), dma((2,)), dma((4,)), dma((4,)),
+            dma(()), dma((4,)), dma((2,)), dma((2,)), dma((2,)), dma((2,)), dma(()), dma((4,)), dma(()), dma(()), dma(()),
         ],
         compiler_params=pltpu.CompilerParams(
             collective_id=0, has_side_effects=True, vmem_limit_bytes=60 * 1024 * 1024

time: 40.6 us -> 40.1 us (0.988)
  Pallas kernels: 39.9 us -> 39.1 us
    pallas_call x1, Pallas kernels: 38.3 us -> 37.6 us  [local(): pl.pallas_call(kernel, name='solves', out_shape=(pltpu.VMEM((STEPS * NB,...]
where the time goes in v8:
time: 40.1 us; the launch traced here: 39.8 us
  Pallas kernels  39.1 us (98%)
  between operations  0.64 us (2%)
    pallas_call x1, Pallas kernels, local(): pl.pallas_call(kernel, name='solves', out_shape=(pltpu.VMEM((STEPS * NB,...  37.6 us
    pallas_call x1, Pallas kernels, local(): pl.pallas_call(hand_over, name='hand_over', out_shape=(jax.ShapeDtypeStru...  1.57 us

profile of v8, /device:TPU:57, one launch (start us, length us, event | category | flops | bytes accessed | tf_op | source)
XLA Modules:
  0.0 39.8 jit_solution(14856110844086384509)
XLA Ops:
  0.6 37.6 %solves.1 = (bf16[3072,256]{1,0:T(8,128)(2,1)S(1)}, f32[16,1024]{1,0:T(8,128)S(1)}, f32[16,1024]{1,0:T(8,128)S(1)}, f32[1024,256]{1,0:T(8,128)S(1)}) custom-call(bf16[1024,1024]{1,0:T(8,128)(2,1)} %factor.1, bf16[1024,1024]{1,0:T(8,128)(2,1)} %inverse.1, bf16[1024,256]{1,0:T(8,128)(2,1)} %rhs.1, bf16[1024,256]{1,0:T(8,128)(2,1)} %start.1), custom_call_target="tpu_custom_call" | custom-call | tf_op jit(solution)/shard_map/solves/pallas_call | solution.py:750
  38.2 1.6 %hand_over.1 = (bf16[3072,256]{1,0:T(8,128)(2,1)}, f32[16,1024]{1,0:T(8,128)}, f32[16,1024]{1,0:T(8,128)}, f32[1024,256]{1,0:T(8,128)}) custom-call(bf16[3072,256]{1,0:T(8,128)(2,1)S(1)} %get-tuple-element.12.refs_0_, f32[16,1024]{1,0:T(8,128)S(1)} %get-tuple-element.13.refs_1_, f32[16,1024]{1,0:T(8,128)S(1)} %get-tuple-element.14.refs_2_, ...), custom_call_target="tpu_custom_call" | custom-call | tf_op jit(solution)/shard_map/hand_over/pallas_call | solution.py:782
